TPU v7x, 512 devices: a whole 4x8x8 slice. The times are simulated.
512 devices in a mesh: dp: 32 (over x, z), sx: 4 (over y_lo), sy: 4 (over y_hi, core).
Axes of the slice: x: 4, y: 8 (y_hi: 2, y_lo: 4; y = y_hi * 4 + y_lo), z: 8, core: 2. Of those that a mesh axis runs over, the one named last changes fastest.
Arguments:
- cotangent: bfloat16 [32, 48, 48, 48, 128], P('dp', 'sx', 'sy'), may hold values from -6 to 6
- spectrum: bfloat16 [2, 32, 8, 8, 4, 128], P(None, 'dp', 'sx', 'sy'), may hold values from -6 to 6
- master: float32 [128, 2, 8, 8, 4, 128], P('dp', None, 'sx', 'sy'), may hold values from -4 to 4
- moment1: float32 [128, 2, 8, 8, 4, 128], P('dp', None, 'sx', 'sy'), may hold values from -24 to 24
- moment2: float32 [128, 2, 8, 8, 4, 128], P('dp', None, 'sx', 'sy'), may hold values from 4 to 256
Outputs:
- input_grad: bfloat16 [32, 48, 48, 48, 128], P('dp', 'sx', 'sy')
- new_master: float32 [128, 2, 8, 8, 4, 128], P('dp', None, 'sx', 'sy')
- new_moment1: float32 [128, 2, 8, 8, 4, 128], P('dp', None, 'sx', 'sy')
- new_moment2: float32 [128, 2, 8, 8, 4, 128], P('dp', None, 'sx', 'sy')
All inputs are finite; a program needn't handle non-finite values.
Results may differ from a plain program's by a relative error of at most 0.0067.
Values may be sent and summed in bfloat16 or wider, within the bound.
No kernel may reach another device: no remote copies, remote signals or barrier semaphores. Data moves between devices by JAX's collectives and lax.ppermute only.
A program may use at most 64 MiB of HBM per device.

v0:
```python
import math

import jax
import jax.numpy as jnp
from jax import lax
from jax.sharding import PartitionSpec as P

NX = 48
NY = 48
NZ = 48
MX = 8
MY = 8
MZ = 4
CO = 128
STEP = 100


exact = lax.Precision.HIGHEST
beta_one = 0.9
beta_two = 0.95
learn_rate = 0.001
epsilon = 1e-08


def mode_numbers(index, count):
    return jnp.where(index < count // 2, index, index - count)


def phase_tables(places, freqs, length):
    product = places[:, None] * freqs[..., None, :] % length
    angle = product.astype(jnp.float32) * (2.0 * math.pi / length)
    return (jnp.cos(angle), jnp.sin(angle))


def analyse(parts, cos_table, sin_table, form):
    real_part = jnp.einsum(form, parts[0], cos_table, precision=exact) + jnp.einsum(
        form, parts[1], sin_table, precision=exact
    )
    imag_part = jnp.einsum(form, parts[1], cos_table, precision=exact) - jnp.einsum(
        form, parts[0], sin_table, precision=exact
    )
    return (real_part, imag_part)


def synthesise(parts, cos_table, sin_table, form):
    real_part = jnp.einsum(form, parts[0], cos_table, precision=exact) - jnp.einsum(
        form, parts[1], sin_table, precision=exact
    )
    imag_part = jnp.einsum(form, parts[0], sin_table, precision=exact) + jnp.einsum(
        form, parts[1], cos_table, precision=exact
    )
    return (real_part, imag_part)


def block_tables(places, blocks, per_block, count, length):
    freqs = mode_numbers(
        blocks[:, None] * per_block + jnp.arange(per_block, dtype=jnp.int32)[None, :], count
    )
    return phase_tables(places, freqs, length)


def shards(cotangent, spectrum, master, moment1, moment2):
    snaps = cotangent.shape[0]
    local_x = cotangent.shape[1]
    local_y = cotangent.shape[2]
    y_devices = lax.axis_size("sy")
    x_modes = MX // lax.axis_size("sx")
    y_modes = MY // y_devices
    x_index = lax.axis_index("sx") * local_x + jnp.arange(local_x, dtype=jnp.int32)
    y_index = lax.axis_index("sy") * local_y + jnp.arange(local_y, dtype=jnp.int32)
    norm = 1.0 / math.sqrt(NX * NY * NZ)
    z_freq = jnp.arange(MZ, dtype=jnp.int32)
    z_cos, z_sin = phase_tables(jnp.arange(NZ, dtype=jnp.int32), z_freq, NZ)
    z_table = jnp.concatenate([z_cos, -z_sin], axis=1).astype(jnp.bfloat16)
    scale = jnp.where(z_freq > 0, 2.0, 1.0).astype(jnp.float32) * norm
    z_part = jnp.einsum("bxyzo,zq->bxyqo", cotangent, z_table, preferred_element_type=jnp.float32)
    z_parts = (z_part[:, :, :, :MZ], z_part[:, :, :, MZ:])
    y_cos, y_sin = phase_tables(y_index, mode_numbers(jnp.arange(MY, dtype=jnp.int32), MY), NY)
    y_parts = analyse(z_parts, y_cos, y_sin, "bxylo,ym->bxmlo")
    blocks = jnp.arange(1 * lax.axis_size(("sx", "sy")), dtype=jnp.int32)
    x_block = blocks // y_devices
    y_block = blocks % y_devices
    chosen_real = jnp.take(
        y_parts[0].reshape(snaps, local_x, y_devices, y_modes, MZ, CO), y_block, axis=2
    )
    chosen_imag = jnp.take(
        y_parts[1].reshape(snaps, local_x, y_devices, y_modes, MZ, CO), y_block, axis=2
    )
    x_cos, x_sin = block_tables(x_index, x_block, x_modes, MX, NX)
    parts = analyse((chosen_real, chosen_imag), x_cos, x_sin, "bxnmlo,nxj->nbjmlo")
    summed = lax.psum_scatter(
        jnp.stack(parts, axis=1), ("sx", "sy"), scatter_dimension=0, tiled=True
    )[0]
    spectral_cot = (summed * scale[:, None]).astype(jnp.bfloat16)
    weight_local = master.astype(jnp.bfloat16)
    cot_real = spectral_cot[0]
    cot_imag = spectral_cot[1]
    piece = lax.all_gather(weight_local, "dp", axis=0, tiled=True)
    weight_real = piece[:, 0]
    weight_imag = piece[:, 1]
    form = "bjmlo,ijmlo->bjmli"
    real_part = jnp.einsum(
        form, cot_real, weight_real, preferred_element_type=jnp.float32
    ) + jnp.einsum(form, cot_imag, weight_imag, preferred_element_type=jnp.float32)
    imag_part = jnp.einsum(
        form, cot_imag, weight_real, preferred_element_type=jnp.float32
    ) - jnp.einsum(form, cot_real, weight_imag, preferred_element_type=jnp.float32)
    mode_grad = jnp.stack([real_part, imag_part]).astype(jnp.bfloat16)
    input_real = spectrum[0]
    input_imag = spectrum[1]
    form = "bjmli,bjmlo->ijmlo"
    real_part = jnp.einsum(
        form, input_real, cot_real, preferred_element_type=jnp.float32
    ) + jnp.einsum(form, input_imag, cot_imag, preferred_element_type=jnp.float32)
    imag_part = jnp.einsum(
        form, input_real, cot_imag, preferred_element_type=jnp.float32
    ) - jnp.einsum(form, input_imag, cot_real, preferred_element_type=jnp.float32)
    weight_grad = lax.psum_scatter(
        jnp.stack([real_part, imag_part], axis=1).astype(jnp.bfloat16),
        "dp",
        scatter_dimension=0,
        tiled=True,
    ).astype(jnp.float32)
    piece = lax.all_gather(mode_grad[None], ("sx", "sy"), axis=0, tiled=True)
    blocks = jnp.arange(piece.shape[0], dtype=jnp.int32)
    x_cos, x_sin = block_tables(x_index, blocks // y_devices, x_modes, MX, NX)
    y_cos, y_sin = block_tables(y_index, blocks % y_devices, y_modes, MY, NY)
    parts = (piece[:, 0].astype(jnp.float32), piece[:, 1].astype(jnp.float32))
    parts = synthesise(parts, x_cos, x_sin, "nbjmli,nxj->nbxmli")
    parts = synthesise(parts, y_cos, y_sin, "nbxmli,nym->bxyli")
    grid_real = parts[0]
    grid_imag = parts[1]
    grid = jnp.einsum("bxyli,zl->bxyzi", grid_real, z_cos, precision=exact) - jnp.einsum(
        "bxyli,zl->bxyzi", grid_imag, z_sin, precision=exact
    )
    input_grad = (grid * norm).astype(jnp.bfloat16)
    new_moment1 = beta_one * moment1 + (1.0 - beta_one) * weight_grad
    new_moment2 = beta_two * moment2 + (1.0 - beta_two) * weight_grad * weight_grad
    first_fix = 1.0 - beta_one**STEP
    second_fix = 1.0 - beta_two**STEP
    new_master = master - learn_rate * (new_moment1 / first_fix) / (
        jnp.sqrt(new_moment2 / second_fix) + epsilon
    )
    return (input_grad, new_master, new_moment1, new_moment2)


def solution(mesh):
    in_specs = (
        P("dp", "sx", "sy", None, None),
        P(None, "dp", "sx", "sy", None, None),
        P("dp", None, "sx", "sy", None, None),
        P("dp", None, "sx", "sy", None, None),
        P("dp", None, "sx", "sy", None, None),
    )
    out_specs = (
        P("dp", "sx", "sy", None, None),
        P("dp", None, "sx", "sy", None, None),
        P("dp", None, "sx", "sy", None, None),
        P("dp", None, "sx", "sy", None, None),
    )
    return jax.shard_map(shards, mesh=mesh, in_specs=in_specs, out_specs=out_specs, check_vma=False)
```

profile of v0, /device:TPU:1, one launch (start us, length us, event | category | flops | bytes accessed | tf_op | source)
XLA Modules:
  0.0 436.3 jit_solution(1192908441580500117)
XLA Ops:
  7.3 0.5 compare_and_fusion
  7.9 0.2 cosine_bitcast_fusion
  8.1 0.1 copy.104
  8.2 0.7 copy.93
  8.8 0.3 fusion.3
  9.2 0.1 slice_bitcast_fusion.3
  9.3 0.4 fusion.30
  9.7 0.4 fusion.26
  10.2 0.4 convolution_add_fusion.1
  10.6 0.4 convolution_subtract_fusion.1
  11.2 1.1 gather_fusion
  12.2 1.2 gather_fusion.1
  13.4 1.1 fusion.19
  14.5 0.7 fusion.16
  15.3 0.7 fusion.12
  16.0 0.7 fusion.11
  16.7 0.7 fusion.10
  17.5 0.1 pad_maximum_fusion.1
  17.6 0.8 copy.75
  18.5 0.2 copy.86
  18.7 0.2 copy.87
  18.9 1.3 dynamic-slice
  20.2 117.6 %all-reduce.5.cloned.1.call-done = f32[16,2,1,2,2,4,128]{6,5,4,3,2,1,0:T(4,128)} async-done(((f32[16,2,1,2,2,4,128]{6,5,4,3,2,1,0:T(4,128)}), f32[16,2,1,2,2,4,128]{6,5,4,3,2,1,0:T(4,128)}) %all-reduce.5.cloned.1.call-update) | async-done | bytes 262160
  137.8 1.4 fusion.44
  139.2 1.4 fusion.24
  140.7 1.6 pad_maximum_fusion
  142.4 1.3 dynamic-slice.2
  144.3 155.4 %all-reduce.7.cloned.1.call-done = bf16[128,2,2,2,4,128]{5,4,3,2,1,0:T(4,128)(2,1)} async-done(((bf16[128,2,2,2,4,128]{5,4,3,2,1,0:T(4,128)(2,1)}), bf16[128,2,2,2,4,128]{5,4,3,2,1,0:T(4,128)(2,1)}) %all-reduce.7.cloned.1.call-update) | async-done | bytes 1048592
  299.7 1.5 divide_subtract_fusion
  301.3 82.1 %all-gather.2.cloned.1.call-done = bf16[128,2,2,2,4,128]{5,4,3,2,1,0:T(4,128)(2,1)} async-done(((bf16[4,2,2,2,4,128]{5,4,3,2,1,0:T(4,128)(2,1)}), bf16[128,2,2,2,4,128]{5,4,3,2,1,0:T(4,128)(2,1)}) %all-gather.2.cloned.1.call-update) | async-done | bytes 1048592 | tf_op jit(solution)/shard_map/all_gather | solution.py:98
  383.4 1.6 slice_bitcast_fusion.1
  385.0 0.5 copy.97
  385.4 0.2 fusion.83
  385.7 0.3 fusion.89
  385.9 0.5 copy.100
  386.4 0.2 fusion.87
  386.6 0.2 fusion.85
  387.0 28.0 %all_gather.7 = bf16[16,2,1,2,2,4,128]{6,3,5,4,0,2,1:T(2,128)(2,1)S(1)} all-gather(bf16[1,2,1,2,2,4,128]{6,3,5,4,0,2,1:T(2,128)(2,1)S(1)} %pad_maximum_fusion.2), channel_id=1, replica_groups=mesh['dp'=32,'sx'=4,'sy'=4] {'sx','sy'}, dimensions={0}, use_global_device_ids=true | all-gather | bytes 139264 | tf_op jit(solution)/shard_map/all_gather | solution.py:124
  414.9 0.7 fusion.37
  415.6 0.7 convolution_add_fusion
  416.3 1.1 convolution_bitcast_fusion
  417.4 1.1 convolution_bitcast_fusion.2
  418.6 0.7 fusion.38
  419.3 0.7 convolution_subtract_fusion
  419.9 1.2 fusion.9
  421.1 1.1 fusion.7
  422.2 3.1 fusion.33
  425.3 4.5 %fusion.2 = bf16[1,12,12,48,128]{4,3,2,1,0:T(8,128)(2,1)} fusion(f32[48,12,12,128]{3,0,2,1:T(8,128)S(1)} %fusion.33, f32[12,12,4,128]{3,1,2,0:T(8,128)S(1)} %fusion.9), kind=kOutput, calls=%fused_computation.5 | convolution fusion | flops 45123264 | bytes 5603328 | tf_op jit(solution)/shard_map/bxyli,zl->bxyzi/dot_general | solution.py:133
  (44 shorter events, 0.5 us)
Async XLA Ops:
  7.2 1.7 copy-start
  7.2 130.6 %all-reduce.5.cloned.1.call-start = ((), (), s32[]{:S(2)}) async-start(), calls=%async_computation.1 | async-start | bytes 524288
  7.8 3.2 copy-start.6
  7.9 4.3 copy-start.9
  13.4 2.6 copy-start.1
  14.5 3.9 copy-start.8
  17.4 282.3 %copy-start.3 = (f32[4,2,2,2,4,128]{5,4,3,2,1,0:T(4,128)S(1)}, f32[4,2,2,2,4,128]{5,4,3,2,1,0:T(4,128)}, u32[]{:S(2)}) copy-start(f32[4,2,2,2,4,128]{5,4,3,2,1,0:T(4,128)} %param.9) | copy-start | bytes 196612
  17.4 282.3 %copy-start.4 = (f32[4,2,2,2,4,128]{5,4,3,2,1,0:T(4,128)S(1)}, f32[4,2,2,2,4,128]{5,4,3,2,1,0:T(4,128)}, u32[]{:S(2)}) copy-start(f32[4,2,2,2,4,128]{5,4,3,2,1,0:T(4,128)} %param.10) | copy-start | bytes 196612
  17.4 282.2 %copy-start.5 = (f32[4,2,2,2,4,128]{5,4,3,2,1,0:T(4,128)S(1)}, f32[4,2,2,2,4,128]{5,4,3,2,1,0:T(4,128)}, u32[]{:S(2)}) copy-start(f32[4,2,2,2,4,128]{5,4,3,2,1,0:T(4,128)} %param.11) | copy-start | bytes 196612
  18.4 281.3 %all-reduce.7.cloned.1.call-start = ((), (), s32[]{:S(2)}) async-start(), calls=%async_computation.2 | async-start | bytes 2097152
  142.3 272.6 %copy-start.2 = (f32[16,12,2,1,1]{1,2,4,3,0:T(2,128)S(1)}, f32[16,12,2,1,1]{1,2,4,3,0:T(2,128)}, u32[]{:S(2)}) copy-start(f32[16,12,2,1,1]{1,2,4,3,0:T(2,128)} %copy.93) | copy-start | bytes 4612
  142.3 241.0 %all-gather.2.cloned.1.call-start = ((), (), s32[]{:S(2)}) async-start(), calls=%async_computation | async-start | bytes 1081344 | tf_op jit(solution)/shard_map/all_gather | solution.py:98
  385.4 30.9 %copy-start.7 = (s32[12]{0:T(128)S(1)}, s32[12]{0:T(128)}, u32[]{:S(2)}) copy-start(s32[12]{0:T(128)} %copy-done.6) | copy-start | bytes 148
Sparse Core Ops, SparseCore 0:
  18.5 119.2 all-reduce.4
  142.5 157.1 all-reduce.6
  303.9 79.4 all-gather.1
where the time goes:
time: 437 us; the launch traced here: 436 us
  waiting for transfers between devices  355 us (81%)
  blocking collectives  28 us (6%)
  matrix products  20.7 us (5%)
  between operations  14.8 us (3%)
  local copies, waits for them, and re-layouts  9.51 us (2%)
  other arithmetic  8.08 us (2%)
    unnamed x5, waiting for transfers between devices  273 us
    all_gather x1, waiting for transfers between devices, shards(): piece = lax.all_gather(weight_local, 'dp', axis=0, tiled=True)  82.1 us
    all_gather x1, blocking collectives, shards(): piece = lax.all_gather(mode_grad[None], ('sx', 'sy'), axis=0, tiled=True)  28 us
  transfers between devices with their start and end apart: 3, of which 3 were waited for; matrix products, arithmetic and copies ran while one was open for 1% of the time, Pallas kernels for 0%

commit v1 on v0

v1 whole, which is shorter than its diff:
```python
import math

import jax
import jax.numpy as jnp
import ml_dtypes
import numpy as np
from jax import lax
from jax.experimental import pallas as pl
from jax.experimental.pallas import tpu as pltpu
from jax.sharding import PartitionSpec as P

NX = 48
NY = 48
NZ = 48
MX = 8
MY = 8
MZ = 4
CI = 128
CO = 128
STEP = 100

beta_one = 0.9
beta_two = 0.95
learn_rate = 0.001
epsilon = 1e-08
norm = 1.0 / math.sqrt(NX * NY * NZ)

LX = 12
LY = 12
CELLS = LY * NZ
ROWS = MY * MZ
MODES = 16
GROUP = 16
SNAPS = 32
OWN = 4
X_STEP = 4

bf16 = jnp.bfloat16
f32 = jnp.float32


def freqs(count):
    index = np.arange(count)
    return np.where(index < count // 2, index, index - count)


def angles(places, numbers, length):
    return 2.0 * np.pi * ((places[:, None] * numbers[None, :]) % length) / length


def narrow(table):
    return table.astype(np.float32).astype(ml_dtypes.bfloat16)


def high_low(table):
    high = narrow(table)
    return high, narrow(table - high.astype(np.float64))


def x_phases():
    theta = angles(np.arange(NX), np.arange(1, 5), NX)
    return np.stack([np.cos(theta), np.sin(theta)], axis=-1).astype(np.float32).reshape(-1)


def analyse_tables():
    z_angle = angles(np.arange(NZ), np.arange(MZ), NZ)
    z_cos = narrow(np.cos(z_angle)).astype(np.float64)
    z_sin = narrow(-np.sin(z_angle)).astype(np.float64)
    y_angle = angles(np.arange(NY), freqs(MY), NY).reshape(4, LY, MY)
    y_cos, y_sin = np.cos(y_angle), np.sin(y_angle)
    real = np.einsum("dym,zl->dmlyz", y_cos, z_cos) + np.einsum("dym,zl->dmlyz", y_sin, z_sin)
    imag = np.einsum("dym,zl->dmlyz", y_cos, z_sin) - np.einsum("dym,zl->dmlyz", y_sin, z_cos)
    table = np.stack([real, imag], axis=1).reshape(4, 2 * ROWS, CELLS)
    return np.concatenate(high_low(table), axis=1)


def synthesise_tables():
    z_angle = angles(np.arange(NZ), np.arange(MZ), NZ)
    y_angle = angles(np.arange(NY), freqs(MY), NY).reshape(4, LY, MY)
    theta = y_angle[:, :, None, :, None] + z_angle[None, None, :, None, :]
    table = norm * np.stack([np.cos(theta), -np.sin(theta)], axis=3)
    high, low = high_low(table.reshape(4, CELLS, 2 * ROWS))
    return np.concatenate([high, low, high], axis=2)


def analyse_kernel(place, cot, table, phase, out, total):
    step = pl.program_id(0)
    tab = table[0]
    real, imag = [], []
    for j in range(0, X_STEP, 2):
        pair = jnp.concatenate([cot[j], cot[j + 1]], axis=1)
        both = jnp.dot(tab, pair, preferred_element_type=f32)
        part = both[: 2 * ROWS] + both[2 * ROWS :]
        for lanes in (slice(0, CO), slice(CO, 2 * CO)):
            real.append(part[:ROWS, lanes])
            imag.append(part[ROWS:, lanes])
    base = (place[0] * LX + step * X_STEP) * 8

    @pl.when(step == 0)
    def _():
        total[...] = jnp.zeros_like(total)

    total[0, 0] += sum(real)
    total[0, 1] += sum(imag)
    for f in range(1, 5):
        rc = rs = ic = is_ = 0.0
        for j in range(X_STEP):
            cos = phase[base + 8 * j + 2 * f - 2]
            sin = phase[base + 8 * j + 2 * f - 1]
            rc += real[j] * cos
            rs += real[j] * sin
            ic += imag[j] * cos
            is_ += imag[j] * sin
        if f < 4:
            total[f, 0] += rc + is_
            total[f, 1] += ic - rs
        total[MX - f, 0] += rc - is_
        total[MX - f, 1] += ic + rs

    @pl.when(step == LX // X_STEP - 1)
    def _():
        for s in range(GROUP):
            x, y = divmod(s, 4)
            for c in range(2):
                block = [total[2 * x + j, c, 8 * y : 8 * y + 8, :] for j in range(2)]
                out[s, :, c * CO : (c + 1) * CO] = jnp.concatenate(block, axis=0).astype(bf16)


def analyse(place, cotangent):
    return pl.pallas_call(
        analyse_kernel,
        out_shape=jax.ShapeDtypeStruct((GROUP, MODES, 2 * CO), bf16),
        grid_spec=pltpu.PrefetchScalarGridSpec(
            num_scalar_prefetch=1,
            grid=(LX // X_STEP,),
            in_specs=[
                pl.BlockSpec((X_STEP, CELLS, CO), lambda i, p: (i, 0, 0)),
                pl.BlockSpec((1, 4 * ROWS, CELLS), lambda i, p: (p[1], 0, 0)),
                pl.BlockSpec(memory_space=pltpu.SMEM),
            ],
            out_specs=pl.BlockSpec((GROUP, MODES, 2 * CO), lambda i, p: (0, 0, 0)),
            scratch_shapes=[pltpu.VMEM((MX, 2, ROWS, CO), f32)],
        ),
        compiler_params=pltpu.CompilerParams(vmem_limit_bytes=24 * 2**20),
        name="analyse",
    )(place, cotangent, jnp.asarray(analyse_tables()), jnp.asarray(x_phases()))


def own_mode(rows, cols):
    row = lax.broadcasted_iota(jnp.int32, (rows, cols), 0) % MODES
    return row == lax.broadcasted_iota(jnp.int32, (rows, cols), 1) % MODES


def channel_of(rows):
    row = lax.broadcasted_iota(jnp.int32, (rows, CI), 0)
    chan = lax.broadcasted_iota(jnp.int32, (rows, CI), 1)
    return jnp.where(chan == (row % SNAPS) * OWN + row // SNAPS, 1.0, 0.0).astype(bf16)


def mix_kernel(cot, master, spec, out):
    rows, cols = SNAPS * MODES, 2 * OWN * MODES
    weight = master[...].reshape(OWN, 2, MODES, CO)
    real, imag = weight[:, 0], weight[:, 1]
    table = jnp.concatenate(
        [
            jnp.stack([real, -imag], axis=1).reshape(cols, CO),
            jnp.stack([imag, real], axis=1).reshape(cols, CO),
        ],
        axis=1,
    ).astype(bf16)
    every = lax.dot_general(
        cot[...].reshape(rows, 2 * CO), table, (((1,), (1,)), ((), ())), preferred_element_type=f32
    )
    grad = jnp.where(own_mode(rows, cols), every, 0.0).reshape(SNAPS, MODES, cols).sum(axis=1)
    turned = lax.dot_general(
        channel_of(OWN * SNAPS), spec[...], (((1,), (1,)), ((), ())), preferred_element_type=f32
    )
    pieces = [turned[i * SNAPS : (i + 1) * SNAPS] for i in range(OWN)]
    out[...] = jnp.concatenate([grad, *pieces], axis=1).astype(bf16)


def mix(cot, master, spec):
    return pl.pallas_call(
        mix_kernel,
        out_shape=jax.ShapeDtypeStruct((SNAPS, 4 * OWN * MODES), bf16),
        in_specs=[pl.BlockSpec(memory_space=pltpu.VMEM)] * 3,
        out_specs=pl.BlockSpec(memory_space=pltpu.VMEM),
        compiler_params=pltpu.CompilerParams(vmem_limit_bytes=24 * 2**20),
        name="mix",
    )(cot, master, spec)


def turn_kernel(got, out):
    width = 2 * MODES
    grad = got[...][:, : OWN * width]
    stacked = jnp.concatenate([grad[:, i * width : (i + 1) * width] for i in range(OWN)], axis=0)
    turned = lax.dot_general(
        stacked, channel_of(OWN * SNAPS), (((0,), (0,)), ((), ())), preferred_element_type=f32
    )
    out[...] = jnp.broadcast_to(turned.astype(bf16)[None], out.shape)


def turn(got):
    return pl.pallas_call(
        turn_kernel,
        out_shape=jax.ShapeDtypeStruct((GROUP, 2 * MODES, CI), bf16),
        in_specs=[pl.BlockSpec(memory_space=pltpu.VMEM)],
        out_specs=pl.BlockSpec(memory_space=pltpu.VMEM),
        compiler_params=pltpu.CompilerParams(vmem_limit_bytes=24 * 2**20),
        name="turn",
    )(got)


def synthesise_kernel(place, modes, table, phase, out, plus, less):
    step = pl.program_id(0)

    @pl.when(step == 0)
    def _():
        parts = [modes[s].astype(f32) for s in range(GROUP)]

        def field(kx, c):
            x, j = divmod(kx, 2)
            at = c * MODES + 8 * j
            return jnp.concatenate([parts[4 * x + y][at : at + 8] for y in range(4)], axis=0)

        for c in range(2):
            plus[0, c] = field(0, c)
            plus[4, c] = field(4, c)
            for f in range(1, 4):
                up, down = field(f, c), field(MX - f, c)
                plus[f, c] = up + down
                less[f, c] = up - down

    base = (place[0] * LX + step * X_STEP) * 8
    tab = table[0]
    for j in range(0, X_STEP, 2):
        pair = []
        for k in (j, j + 1):
            real, imag = plus[0, 0], plus[0, 1]
            for f in range(1, 5):
                cos = phase[base + 8 * k + 2 * f - 2]
                sin = phase[base + 8 * k + 2 * f - 1]
                if f < 4:
                    real += plus[f, 0] * cos - less[f, 1] * sin
                    imag += plus[f, 1] * cos + less[f, 0] * sin
                else:
                    real += plus[4, 0] * cos + plus[4, 1] * sin
                    imag += plus[4, 1] * cos - plus[4, 0] * sin
            field_ = jnp.concatenate([real, imag], axis=0)
            high = field_.astype(bf16)
            low = (field_ - high.astype(f32)).astype(bf16)
            pair.append(jnp.concatenate([high, high, low], axis=0))
        both = jnp.dot(tab, jnp.concatenate(pair, axis=1), preferred_element_type=f32)
        both = both.astype(bf16)
        out[j] = both[:, :CI]
        out[j + 1] = both[:, CI:]


def synthesise(place, modes):
    return pl.pallas_call(
        synthesise_kernel,
        out_shape=jax.ShapeDtypeStruct((LX, CELLS, CI), bf16),
        grid_spec=pltpu.PrefetchScalarGridSpec(
            num_scalar_prefetch=1,
            grid=(LX // X_STEP,),
            in_specs=[
                pl.BlockSpec((GROUP, 2 * MODES, CI), lambda i, p: (0, 0, 0)),
                pl.BlockSpec((1, CELLS, 6 * ROWS), lambda i, p: (p[1], 0, 0)),
                pl.BlockSpec(memory_space=pltpu.SMEM),
            ],
            out_specs=pl.BlockSpec((X_STEP, CELLS, CI), lambda i, p: (i, 0, 0)),
            scratch_shapes=[
                pltpu.VMEM((5, 2, ROWS, CI), f32),
                pltpu.VMEM((4, 2, ROWS, CI), f32),
            ],
        ),
        compiler_params=pltpu.CompilerParams(vmem_limit_bytes=24 * 2**20),
        name="synthesise",
    )(place, modes, jnp.asarray(synthesise_tables()), jnp.asarray(x_phases()))


def adam_kernel(cot, got, master, moment1, moment2, new_master, new_moment1, new_moment2):
    rows, cols = SNAPS * MODES, 2 * OWN * MODES
    spec = got[...][:, cols:].astype(f32)
    spread = jnp.broadcast_to(spec[:, None, :], (SNAPS, MODES, cols)).reshape(rows, cols)
    spread = jnp.where(own_mode(rows, cols), spread, 0.0).astype(bf16)
    products = lax.dot_general(
        spread, cot[...].reshape(rows, 2 * CO), (((0,), (0,)), ((), ())), preferred_element_type=f32
    ).reshape(OWN, 2, MODES, 2 * CO)
    real = products[:, 0, :, :CO] + products[:, 1, :, CO:]
    imag = products[:, 0, :, CO:] - products[:, 1, :, :CO]
    grad = jnp.stack([real, imag], axis=1).reshape(cols, CO)
    first = beta_one * moment1[...] + (1.0 - beta_one) * grad
    second = beta_two * moment2[...] + (1.0 - beta_two) * grad * grad
    first_fix = 1.0 - beta_one**STEP
    second_fix = 1.0 - beta_two**STEP
    new_moment1[...] = first
    new_moment2[...] = second
    new_master[...] = master[...] - learn_rate * (first / first_fix) / (
        jnp.sqrt(second / second_fix) + epsilon
    )


def adam(cot, got, master, moment1, moment2):
    whole = pl.BlockSpec(memory_space=pltpu.VMEM)
    return pl.pallas_call(
        adam_kernel,
        out_shape=[jax.ShapeDtypeStruct(master.shape, f32)] * 3,
        in_specs=[whole] * 5,
        out_specs=[whole] * 3,
        compiler_params=pltpu.CompilerParams(vmem_limit_bytes=24 * 2**20),
        name="adam",
    )(cot, got, master, moment1, moment2)


def shards(cotangent, spectrum, master, moment1, moment2):
    place = jnp.stack([lax.axis_index("sx"), lax.axis_index("sy")]).astype(jnp.int32)
    partial = analyse(place, cotangent.reshape(LX, CELLS, CO))
    partial = lax.all_to_all(partial, ("sx", "sy"), 0, 0, tiled=True)
    scale = norm * np.tile(np.array([1.0, 2.0, 2.0, 2.0], np.float32), MODES // MZ)
    spectral_cot = (partial.astype(f32).sum(axis=0) * scale[:, None]).astype(bf16)
    every_cot = jnp.broadcast_to(spectral_cot[None], (SNAPS, MODES, 2 * CO))
    every_cot = lax.all_to_all(every_cot, "dp", 0, 0, tiled=True)
    state = (2 * OWN * MODES, CO)
    weight = master.reshape(state)
    got = mix(every_cot, weight, spectrum.reshape(2 * MODES, CI))
    got = lax.all_to_all(got, "dp", 0, 0, tiled=True)
    modes = lax.all_to_all(turn(got), ("sx", "sy"), 0, 0, tiled=True)
    input_grad = synthesise(place, modes).reshape(cotangent.shape)
    states = adam(every_cot, got, weight, moment1.reshape(state), moment2.reshape(state))
    return (input_grad, *(s.reshape(master.shape) for s in states))


def solution(mesh):
    grid = P("dp", "sx", "sy", None, None)
    state = P("dp", None, "sx", "sy", None, None)
    in_specs = (grid, P(None, "dp", "sx", "sy", None, None), state, state, state)
    out_specs = (grid, state, state, state)
    return jax.shard_map(shards, mesh=mesh, in_specs=in_specs, out_specs=out_specs, check_vma=False)
```

time: 437 us -> 82.8 us (0.19)
  waiting for transfers between devices: 355 us -> 8.04 us
  blocking collectives: 28 us -> 55.3 us
  matrix products: 20.7 us -> 0 us
  between operations: 14.8 us -> 0.73 us
  Pallas kernels: 0 us -> 7.95 us
  other arithmetic: 8.08 us -> 0.82 us
  local copies, waits for them, and re-layouts: 9.51 us -> 3.85 us
  starting transfers between devices: 0.12 us -> 5.66 us
    unnamed x5 -> x0, waiting for transfers between devices: 273 us -> none
    all_gather x1 -> x0, waiting for transfers between devices: 82.1 us -> none  [shards(): piece = lax.all_gather(weight_local, 'dp', axis=0, tiled=True)]
    all_to_all x0 -> x3, blocking collectives: none -> 55.3 us  [the longest x1 22.3 us: shards(): every_cot = lax.all_to_all(every_cot, 'dp', 0, 0, tiled=True)]
    all_gather x1 -> x0, blocking collectives: 28 us -> none  [shards(): piece = lax.all_gather(mode_grad[None], ('sx', 'sy'), axis=0, tiled=True)]
    dot_general x23 -> x0, matrix products: 20.7 us -> none  [the longest x1 4.48 us: shards(): jnp.einsum('bxyli,zl->bxyzi', grid_imag, z_sin, precision=exact)]
    all_to_all x0 -> x1, waiting for transfers between devices: none -> 8.04 us  [shards(): modes = lax.all_to_all(turn(got), ('sx', 'sy'), 0, 0, tiled=True)]
    pallas_call x0 -> x5, Pallas kernels: none -> 7.95 us  [the longest x1 3.55 us: synthesise(): pl.pallas_call(synthesise_kernel, out_shape=jax.ShapeDtypeStruct((LX, CEL...]
    all_to_all x0 -> x1, starting transfers between devices: none -> 5.66 us  [shards(): modes = lax.all_to_all(turn(got), ('sx', 'sy'), 0, 0, tiled=True)]
  transfers between devices with their start and end apart: 3 -> 1, of which waited for: 3 -> 1; matrix products, arithmetic and copies ran while one was open for 1% -> 0% of each run, Pallas kernels for 0% -> 1%
where the time goes in v1:
time: 82.8 us; the launch traced here: 82.4 us
  blocking collectives  55.3 us (67%)
  waiting for transfers between devices  8.04 us (10%)
  Pallas kernels  7.95 us (10%)
  starting transfers between devices  5.66 us (7%)
  local copies, waits for them, and re-layouts  3.85 us (5%)
    all_to_all x1, blocking collectives, shards(): every_cot = lax.all_to_all(every_cot, 'dp', 0, 0, tiled=True)  22.3 us
    all_to_all x1, blocking collectives, shards(): partial = lax.all_to_all(partial, ('sx', 'sy'), 0, 0, tiled=True)  18.4 us
    all_to_all x1, blocking collectives, shards(): got = lax.all_to_all(got, 'dp', 0, 0, tiled=True)  14.6 us
    all_to_all x1, waiting for transfers between devices, shards(): modes = lax.all_to_all(turn(got), ('sx', 'sy'), 0, 0, tiled=True)  8.04 us
    all_to_all x1, starting transfers between devices, shards(): modes = lax.all_to_all(turn(got), ('sx', 'sy'), 0, 0, tiled=True)  5.66 us
    pallas_call x1, Pallas kernels, synthesise(): pl.pallas_call(synthesise_kernel, out_shape=jax.ShapeDtypeStruct((LX, CEL...  3.55 us
    unnamed x23, local copies, waits for them, and re-layouts  3.31 us
    pallas_call x1, Pallas kernels, analyse(): pl.pallas_call(analyse_kernel, out_shape=jax.ShapeDtypeStruct((GROUP, MOD...  2.25 us
  transfers between devices with their start and end apart: 1, of which 1 were waited for; matrix products, arithmetic and copies ran while one was open for 0% of the time, Pallas kernels for 1%

profile of v1, /device:TPU:1, one launch (start us, length us, event | category | flops | bytes accessed | tf_op | source)
XLA Modules:
  0.0 82.4 jit_solution(8516929772414756676)
XLA Ops:
  0.6 0.0 copy-start.9
  0.6 0.1 pad_add_fusion.place
  0.7 0.0 copy-start
  0.7 1.5 %copy-done = bf16[1,12,12,48,128]{4,3,2,1,0:T(8,128)(2,1)S(1)} copy-done((bf16[1,12,12,48,128]{4,3,2,1,0:T(8,128)(2,1)S(1)}, bf16[1,12,12,48,128]{4,3,2,1,0:T(8,128)(2,1)}, u32[]{:S(2)}) %copy-start) | copy-done | bytes 1769496
  2.2 0.0 copy-start.2
  2.2 1.1 %copy-done.2 = bf16[4,128,576]{2,1,0:T(8,128)(2,1)S(1)} copy-done((bf16[4,128,576]{2,1,0:T(8,128)(2,1)S(1)}, bf16[4,128,576]{2,1,0:T(8,128)(2,1)}, u32[]{:S(2)}) %copy-start.2) | copy-done | bytes 589848
  3.3 0.0 copy-start.7
  3.3 0.7 copy-done.7
  4.0 0.0 copy-start.3
  4.0 0.0 copy-start.6
  4.0 0.0 copy-start.4
  4.0 0.0 copy-start.5
  4.0 2.3 %analyse.1 = bf16[16,16,256]{2,1,0:T(8,128)(2,1)S(1)} custom-call(s32[2]{0:T(128)S(1)} %pad_add_fusion.place, bf16[12,576,128]{2,1,0:T(8,128)(2,1)S(1)} %bitcast.15, bf16[4,128,576]{2,1,0:T(8,128)(2,1)S(1)} %copy-done.2, f32[384]{0:T(512)S(1)} %copy-done.7), custom_call_target="tpu_custom_call" | custom-call | tf_op jit(solution)/shard_map/analyse/pallas_call | solution.py:130
  6.2 0.0 copy-start.1
  6.3 0.0 copy-start.8
  6.3 18.4 %all_to_all.26 = bf16[16,16,256]{2,1,0:T(8,128)(2,1)S(1)} all-to-all(bf16[16,16,256]{2,1,0:T(8,128)(2,1)S(1)} %analyse.1), channel_id=1, replica_groups=mesh['dp'=32,'sx'=4,'sy'=4] {'sx','sy'}, dimensions={0} | all-to-all | bytes 262144 | tf_op jit(solution)/shard_map/all_to_all | solution.py:319
  24.7 0.0 copy-done.9
  24.7 0.1 multiply_convert_fusion
  24.8 22.3 %all_to_all.27.cot = bf16[32,16,256]{2,1,0:T(8,128)(2,1)S(1)} all-to-all(bf16[32,16,256]{2,1,0:T(8,128)(2,1)S(1)} %broadcast_in_dim.2), channel_id=1, replica_groups=mesh['dp'=32,'sx'=4,'sy'=4] {'dp'}, dimensions={0} | all-to-all | bytes 524288 | tf_op jit(solution)/shard_map/all_to_all | solution.py:323
  47.1 0.0 copy-done.3
  47.1 0.0 copy-done.6
  47.1 0.3 mix.1
  47.4 0.5 broadcast.6
  47.9 0.7 reduce
  48.6 14.6 %all_to_all.28 = bf16[32,2,128]{2,1,0:T(2,128)(2,1)S(1)} all-to-all(bf16[32,2,128]{2,1,0:T(2,128)(2,1)S(1)} %reshape.63), channel_id=1, replica_groups=mesh['dp'=32,'sx'=4,'sy'=4] {'dp'}, dimensions={0} | all-to-all | bytes 32768 | tf_op jit(solution)/shard_map/all_to_all | solution.py:327
  63.3 0.9 %turn.1 = bf16[16,32,128]{2,1,0:T(8,128)(2,1)} custom-call(bf16[32,256]{1,0:T(8,128)(2,1)S(1)} %bitcast.18), custom_call_target="tpu_custom_call" | custom-call | tf_op jit(solution)/shard_map/turn/pallas_call | solution.py:204
  64.2 5.7 %all-to-all-start.3 = ((bf16[16,32,128]{2,1,0:T(8,128)(2,1)}), bf16[16,32,128]{2,1,0:T(8,128)(2,1)S(1)}, u32[]{:S(2)}, u32[]{:S(2)}) async-start(bf16[16,32,128]{2,1,0:T(8,128)(2,1)} %turn.1), calls=%async_computation.3 | async-start | bytes 262144 | tf_op jit(solution)/shard_map/all_to_all | solution.py:328
  69.8 0.0 copy-done.4
  69.8 0.0 copy-done.5
  69.8 0.9 %adam.1 = (f32[128,128]{1,0:T(8,128)}, f32[128,128]{1,0:T(8,128)}, f32[128,128]{1,0:T(8,128)}) custom-call(bf16[32,16,256]{2,1,0:T(8,128)(2,1)S(1)} %all_to_all.27.cot, bf16[32,256]{1,0:T(8,128)(2,1)S(1)} %bitcast.19, f32[128,128]{1,0:T(8,128)S(1)} %bitcast.17, f32[128,128]{1,0:T(8,128)S(1)} %bitcast.21, f32[128,128]{1,0:T(8,128)S(1)} %bitcast.22), custom_call_target="tpu_custom_call" | custom-call | tf_op jit(solution)/shard_map/adam/pallas_call | solution.py:306
  70.8 8.0 %all-to-all-done.3.modes = bf16[16,32,128]{2,1,0:T(8,128)(2,1)S(1)} async-done(((bf16[16,32,128]{2,1,0:T(8,128)(2,1)}), bf16[16,32,128]{2,1,0:T(8,128)(2,1)S(1)}, u32[]{:S(2)}, u32[]{:S(2)}) %all-to-all-start.3) | async-done | bytes 131104 | tf_op jit(solution)/shard_map/all_to_all | solution.py:328
  78.8 0.0 copy-done.1
  78.8 0.0 copy-done.8
  78.8 3.5 %synthesise.1 = bf16[12,576,128]{2,1,0:T(8,128)(2,1)} custom-call(s32[2]{0:T(128)S(1)} %pad_add_fusion.place, bf16[16,32,128]{2,1,0:T(8,128)(2,1)S(1)} %all-to-all-done.3.modes, bf16[4,576,192]{2,1,0:T(8,128)(2,1)S(1)} %copy-done.1, f32[384]{0:T(512)S(1)} %copy-done.8), custom_call_target="tpu_custom_call" | custom-call | tf_op jit(solution)/shard_map/synthesise/pallas_call | solution.py:260
  (5 shorter events, 0.1 us)
Async XLA Ops:
  0.6 24.1 %copy-start.9 = (f32[16]{0:T(128)S(1)}, f32[16]{0:T(128)}, u32[]{:S(2)}) copy-start(f32[16]{0:T(128)} %constant.26) | copy-start | bytes 196
  0.7 1.5 %copy-start = (bf16[1,12,12,48,128]{4,3,2,1,0:T(8,128)(2,1)S(1)}, bf16[1,12,12,48,128]{4,3,2,1,0:T(8,128)(2,1)}, u32[]{:S(2)}) copy-start(bf16[1,12,12,48,128]{4,3,2,1,0:T(8,128)(2,1)} %param.10) | copy-start | bytes 5308420
  2.2 1.1 %copy-start.2 = (bf16[4,128,576]{2,1,0:T(8,128)(2,1)S(1)}, bf16[4,128,576]{2,1,0:T(8,128)(2,1)}, u32[]{:S(2)}) copy-start(bf16[4,128,576]{2,1,0:T(8,128)(2,1)} %constant.17.clone.table) | copy-start | bytes 1769476
  3.3 0.7 copy-start.7
  4.0 43.1 %copy-start.3 = (f32[4,2,2,2,4,128]{5,4,3,2,1,0:T(4,128)S(1)}, f32[4,2,2,2,4,128]{5,4,3,2,1,0:T(4,128)}, u32[]{:S(2)}) copy-start(f32[4,2,2,2,4,128]{5,4,3,2,1,0:T(4,128)} %param.12) | copy-start | bytes 196612
  4.0 43.1 %copy-start.6 = (bf16[2,1,2,2,4,128]{5,4,3,2,1,0:T(4,128)(2,1)S(1)}, bf16[2,1,2,2,4,128]{5,4,3,2,1,0:T(4,128)(2,1)}, u32[]{:S(2)}) copy-start(bf16[2,1,2,2,4,128]{5,4,3,2,1,0:T(4,128)(2,1)} %param.11) | copy-start | bytes 24580
  4.0 65.8 %copy-start.4 = (f32[4,2,2,2,4,128]{5,4,3,2,1,0:T(4,128)S(1)}, f32[4,2,2,2,4,128]{5,4,3,2,1,0:T(4,128)}, u32[]{:S(2)}) copy-start(f32[4,2,2,2,4,128]{5,4,3,2,1,0:T(4,128)} %param.13) | copy-start | bytes 196612
  4.0 65.9 %copy-start.5 = (f32[4,2,2,2,4,128]{5,4,3,2,1,0:T(4,128)S(1)}, f32[4,2,2,2,4,128]{5,4,3,2,1,0:T(4,128)}, u32[]{:S(2)}) copy-start(f32[4,2,2,2,4,128]{5,4,3,2,1,0:T(4,128)} %param.14) | copy-start | bytes 196612
  6.2 72.6 %copy-start.1 = (bf16[4,576,192]{2,1,0:T(8,128)(2,1)S(1)}, bf16[4,576,192]{2,1,0:T(8,128)(2,1)}, u32[]{:S(2)}) copy-start(bf16[4,576,192]{2,1,0:T(8,128)(2,1)} %constant.20.clone.table) | copy-start | bytes 2654212
  6.3 72.6 %copy-start.8 = (f32[384]{0:T(512)S(1)}, f32[384]{0:T(512)}, u32[]{:S(2)}) copy-start(f32[384]{0:T(512)} %constant.18.clone.phase) | copy-start | bytes 4612
  64.2 14.7 %all-to-all-start.3 = ((bf16[16,32,128]{2,1,0:T(8,128)(2,1)}), bf16[16,32,128]{2,1,0:T(8,128)(2,1)S(1)}, u32[]{:S(2)}, u32[]{:S(2)}) async-start(bf16[16,32,128]{2,1,0:T(8,128)(2,1)} %turn.1), calls=%async_computation.3 | async-start | bytes 262144 | tf_op jit(solution)/shard_map/all_to_all | solution.py:328

commit v2 on v1

v2 whole, which is shorter than its diff:
```python
import math

import jax
import jax.numpy as jnp
import ml_dtypes
import numpy as np
from jax import lax
from jax.experimental import pallas as pl
from jax.experimental.pallas import tpu as pltpu
from jax.sharding import PartitionSpec as P

NX = 48
NY = 48
NZ = 48
MX = 8
MY = 8
MZ = 4
CI = 128
CO = 128
STEP = 100

beta_one = 0.9
beta_two = 0.95
learn_rate = 0.001
epsilon = 1e-08
norm = 1.0 / math.sqrt(NX * NY * NZ)

LX = 12
LY = 12
CELLS = LY * NZ
ROWS = MY * MZ
MODES = 16
GROUP = 16
SNAPS = 32
OWN = 4
CHUNK = 4

bf16 = jnp.bfloat16
f32 = jnp.float32


def freqs(count):
    index = np.arange(count)
    return np.where(index < count // 2, index, index - count)


def angles(places, numbers, length):
    return 2.0 * np.pi * ((places[:, None] * numbers[None, :]) % length) / length


def narrow(table):
    return table.astype(np.float32).astype(ml_dtypes.bfloat16)


def high_low(table):
    high = narrow(table)
    return high, narrow(table - high.astype(np.float64))


def x_phase(f, x):
    theta = 2.0 * math.pi * (f * x % NX) / NX
    return math.cos(theta), math.sin(theta)


def analyse_table():
    z_angle = angles(np.arange(NZ), np.arange(MZ), NZ)
    z_cos = narrow(np.cos(z_angle)).astype(np.float64)
    z_sin = narrow(-np.sin(z_angle)).astype(np.float64)
    y_angle = angles(np.arange(LY), freqs(MY), NY)
    y_cos, y_sin = np.cos(y_angle), np.sin(y_angle)
    real = np.einsum("ym,zl->mlyz", y_cos, z_cos) + np.einsum("ym,zl->mlyz", y_sin, z_sin)
    imag = np.einsum("ym,zl->mlyz", y_cos, z_sin) - np.einsum("ym,zl->mlyz", y_sin, z_cos)
    return np.concatenate(high_low(np.stack([real, imag]).reshape(2 * ROWS, CELLS)), axis=0)


def synthesise_table():
    z_angle = angles(np.arange(NZ), np.arange(MZ), NZ)
    y_angle = angles(np.arange(LY), freqs(MY), NY)
    theta = y_angle[:, None, :, None] + z_angle[None, :, None, :]
    table = norm * np.stack([np.cos(theta), -np.sin(theta)], axis=2)
    high, low = high_low(table.reshape(CELLS, 2 * ROWS))
    return np.concatenate([high, low, high], axis=1)


def quarter_turns(place, kx):
    row = lax.broadcasted_iota(jnp.int32, (ROWS, CO), 0) // MZ
    ky = jnp.where(row < MY // 2, row, row - MY)
    turns = (ky * place[1] + int(freqs(MX)[kx]) * place[0]) & 3
    cos = jnp.where(turns == 0, 1.0, jnp.where(turns == 2, -1.0, 0.0))
    sin = jnp.where(turns == 1, 1.0, jnp.where(turns == 3, -1.0, 0.0))
    return cos, sin


def analyse_kernel(place, cot_hbm, table_hbm, out, cot, table, total, sems):
    chunks = LX // CHUNK
    copies = [pltpu.make_async_copy(table_hbm, table, sems.at[chunks])]
    for n in range(chunks):
        part = pl.ds(n * CHUNK, CHUNK)
        copies.append(pltpu.make_async_copy(cot_hbm.at[part], cot.at[part], sems.at[n]))
    for copy in copies:
        copy.start()
    copies[0].wait()
    for n in range(chunks):
        copies[1 + n].wait()
        real, imag = [], []
        for x in range(n * CHUNK, (n + 1) * CHUNK, 2):
            pair = jnp.concatenate([cot[x], cot[x + 1]], axis=1)
            both = jnp.dot(table[...], pair, preferred_element_type=f32)
            part = both[: 2 * ROWS] + both[2 * ROWS :]
            for lanes in (slice(0, CO), slice(CO, 2 * CO)):
                real.append(part[:ROWS, lanes])
                imag.append(part[ROWS:, lanes])

        def add(kx, c, value, n=n):
            total[kx, c] = value if n == 0 else total[kx, c] + value

        add(0, 0, sum(real))
        add(0, 1, sum(imag))
        for f in range(1, 5):
            rc = rs = ic = is_ = 0.0
            for j in range(CHUNK):
                cos, sin = x_phase(f, n * CHUNK + j)
                rc += real[j] * cos
                rs += real[j] * sin
                ic += imag[j] * cos
                is_ += imag[j] * sin
            if f < 4:
                add(f, 0, rc + is_)
                add(f, 1, ic - rs)
            add(MX - f, 0, rc - is_)
            add(MX - f, 1, ic + rs)
    for x in range(4):
        halves = []
        for j in range(2):
            cos, sin = quarter_turns(place, 2 * x + j)
            real, imag = total[2 * x + j, 0], total[2 * x + j, 1]
            halves.append((real * cos + imag * sin, imag * cos - real * sin))
        for y in range(4):
            for c in range(2):
                block = [half[c][8 * y : 8 * y + 8] for half in halves]
                out[4 * x + y, :, c * CO : (c + 1) * CO] = jnp.concatenate(block, axis=0).astype(bf16)


def in_hbm(array):
    return pltpu.with_memory_space_constraint(array, pltpu.HBM)


def analyse(place, cotangent):
    return pl.pallas_call(
        analyse_kernel,
        out_shape=jax.ShapeDtypeStruct((GROUP, MODES, 2 * CO), bf16),
        in_specs=[
            pl.BlockSpec(memory_space=pltpu.SMEM),
            pl.BlockSpec(memory_space=pltpu.HBM),
            pl.BlockSpec(memory_space=pltpu.HBM),
        ],
        out_specs=pl.BlockSpec(memory_space=pltpu.VMEM),
        scratch_shapes=[
            pltpu.VMEM((LX, CELLS, CO), bf16),
            pltpu.VMEM((4 * ROWS, CELLS), bf16),
            pltpu.VMEM((MX, 2, ROWS, CO), f32),
            pltpu.SemaphoreType.DMA((LX // CHUNK + 1,)),
        ],
        compiler_params=pltpu.CompilerParams(vmem_limit_bytes=24 * 2**20),
        name="analyse",
    )(place, in_hbm(cotangent), in_hbm(jnp.asarray(analyse_table())))


def own_mode(rows, cols):
    row = lax.broadcasted_iota(jnp.int32, (rows, cols), 0) % MODES
    return row == lax.broadcasted_iota(jnp.int32, (rows, cols), 1) % MODES


def channel_of(rows):
    row = lax.broadcasted_iota(jnp.int32, (rows, CI), 0)
    chan = lax.broadcasted_iota(jnp.int32, (rows, CI), 1)
    return jnp.where(chan == (row % SNAPS) * OWN + row // SNAPS, 1.0, 0.0).astype(bf16)


def mix_kernel(cot, master, spec, out):
    rows, cols = SNAPS * MODES, 2 * OWN * MODES
    weight = master[...].reshape(OWN, 2, MODES, CO)
    real, imag = weight[:, 0], weight[:, 1]
    table = jnp.concatenate(
        [
            jnp.stack([real, -imag], axis=1).reshape(cols, CO),
            jnp.stack([imag, real], axis=1).reshape(cols, CO),
        ],
        axis=1,
    ).astype(bf16)
    every = lax.dot_general(
        cot[...].reshape(rows, 2 * CO), table, (((1,), (1,)), ((), ())), preferred_element_type=f32
    )
    grad = jnp.where(own_mode(rows, cols), every, 0.0).reshape(SNAPS, MODES, cols).sum(axis=1)
    turned = lax.dot_general(
        channel_of(OWN * SNAPS), spec[...], (((1,), (1,)), ((), ())), preferred_element_type=f32
    )
    pieces = [turned[i * SNAPS : (i + 1) * SNAPS] for i in range(OWN)]
    out[:, 0, :] = grad.astype(bf16)
    out[:, 1, :] = jnp.concatenate(pieces, axis=1).astype(bf16)


def mix(cot, master, spec):
    return pl.pallas_call(
        mix_kernel,
        out_shape=jax.ShapeDtypeStruct((SNAPS, 2, 2 * OWN * MODES), bf16),
        in_specs=[pl.BlockSpec(memory_space=pltpu.VMEM)] * 3,
        out_specs=pl.BlockSpec(memory_space=pltpu.VMEM),
        compiler_params=pltpu.CompilerParams(vmem_limit_bytes=24 * 2**20),
        name="mix",
    )(cot, master, spec)


def turn_kernel(got, out):
    width = 2 * MODES
    grad = got[:, 0, :]
    stacked = jnp.concatenate([grad[:, i * width : (i + 1) * width] for i in range(OWN)], axis=0)
    turned = lax.dot_general(
        stacked, channel_of(OWN * SNAPS), (((0,), (0,)), ((), ())), preferred_element_type=f32
    )
    out[...] = jnp.broadcast_to(turned.astype(bf16)[None], out.shape)


def turn(got):
    return pl.pallas_call(
        turn_kernel,
        out_shape=jax.ShapeDtypeStruct((GROUP, 2 * MODES, CI), bf16),
        in_specs=[pl.BlockSpec(memory_space=pltpu.VMEM)],
        out_specs=pl.BlockSpec(memory_space=pltpu.VMEM),
        compiler_params=pltpu.CompilerParams(vmem_limit_bytes=24 * 2**20),
        name="turn",
    )(got)


def adam_step(cot, got, master, moment1, moment2):
    rows, cols = SNAPS * MODES, 2 * OWN * MODES
    spec = got[:, 1, :].astype(f32)
    spread = jnp.broadcast_to(spec[:, None, :], (SNAPS, MODES, cols)).reshape(rows, cols)
    spread = jnp.where(own_mode(rows, cols), spread, 0.0).astype(bf16)
    products = lax.dot_general(
        spread, cot[...].reshape(rows, 2 * CO), (((0,), (0,)), ((), ())), preferred_element_type=f32
    ).reshape(OWN, 2, MODES, 2 * CO)
    real = products[:, 0, :, :CO] + products[:, 1, :, CO:]
    imag = products[:, 0, :, CO:] - products[:, 1, :, :CO]
    grad = jnp.stack([real, imag], axis=1).reshape(cols, CO)
    first = beta_one * moment1[...] + (1.0 - beta_one) * grad
    second = beta_two * moment2[...] + (1.0 - beta_two) * grad * grad
    first_fix = 1.0 - beta_one**STEP
    second_fix = 1.0 - beta_two**STEP
    stepped = master[...] - learn_rate * (first / first_fix) / (
        jnp.sqrt(second / second_fix) + epsilon
    )
    return stepped, first, second


def finish_kernel(place, modes, table, cot, got, master, moment1, moment2, *refs):
    out_hbm, *states_hbm = refs[:4]
    out, states, plus, less, sems = refs[4:]
    parts = [modes[s].astype(f32) for s in range(GROUP)]

    def field(kx):
        x, j = divmod(kx, 2)
        real, imag = (
            jnp.concatenate(
                [parts[4 * x + y][c * MODES + 8 * j : c * MODES + 8 * j + 8] for y in range(4)], axis=0
            )
            for c in range(2)
        )
        cos, sin = quarter_turns(place, kx)
        return real * cos - imag * sin, imag * cos + real * sin

    for f in range(5):
        up = field(f)
        for c in range(2):
            plus[f, c] = up[c]
        if 0 < f < 4:
            down = field(MX - f)
            for c in range(2):
                plus[f, c] = up[c] + down[c]
                less[f, c] = up[c] - down[c]
    copies = []
    for x in range(0, LX, 2):
        pair = []
        for k in (x, x + 1):
            real, imag = plus[0, 0], plus[0, 1]
            for f in range(1, 5):
                cos, sin = x_phase(f, k)
                if f < 4:
                    real += plus[f, 0] * cos - less[f, 1] * sin
                    imag += plus[f, 1] * cos + less[f, 0] * sin
                else:
                    real += plus[4, 0] * cos + plus[4, 1] * sin
                    imag += plus[4, 1] * cos - plus[4, 0] * sin
            both = jnp.concatenate([real, imag], axis=0)
            high = both.astype(bf16)
            low = (both - high.astype(f32)).astype(bf16)
            pair.append(jnp.concatenate([high, high, low], axis=0))
        cells = jnp.dot(table[...], jnp.concatenate(pair, axis=1), preferred_element_type=f32)
        cells = cells.astype(bf16)
        out[x] = cells[:, :CI]
        out[x + 1] = cells[:, CI:]
        part = pl.ds(x, 2)
        copies.append(pltpu.make_async_copy(out.at[part], out_hbm.at[part], sems.at[x // 2]))
        copies[-1].start()
    for n, state in enumerate(adam_step(cot, got, master, moment1, moment2)):
        states[n] = state
        copies.append(pltpu.make_async_copy(states.at[n], states_hbm[n], sems.at[LX // 2 + n]))
        copies[-1].start()
    for copy in copies:
        copy.wait()


def finish(place, modes, cot, got, master, moment1, moment2):
    state = jax.ShapeDtypeStruct(master.shape, f32)
    return pl.pallas_call(
        finish_kernel,
        out_shape=[jax.ShapeDtypeStruct((LX, CELLS, CI), bf16), state, state, state],
        in_specs=[pl.BlockSpec(memory_space=pltpu.SMEM)]
        + [pl.BlockSpec(memory_space=pltpu.VMEM)] * 7,
        out_specs=[pl.BlockSpec(memory_space=pltpu.HBM)] * 4,
        scratch_shapes=[
            pltpu.VMEM((LX, CELLS, CI), bf16),
            pltpu.VMEM((3,) + master.shape, f32),
            pltpu.VMEM((5, 2, ROWS, CI), f32),
            pltpu.VMEM((4, 2, ROWS, CI), f32),
            pltpu.SemaphoreType.DMA((LX // 2 + 3,)),
        ],
        compiler_params=pltpu.CompilerParams(vmem_limit_bytes=24 * 2**20),
        name="finish",
    )(place, modes, jnp.asarray(synthesise_table()), cot, got, master, moment1, moment2)


def shards(cotangent, spectrum, master, moment1, moment2):
    place = jnp.stack([lax.axis_index("sx"), lax.axis_index("sy")]).astype(jnp.int32)
    partial = analyse(place, cotangent.reshape(LX, CELLS, CO))
    partial = lax.all_to_all(partial, ("sx", "sy"), 0, 0, tiled=True)
    scale = norm * np.tile(np.array([1.0, 2.0, 2.0, 2.0], np.float32), MODES // MZ)
    spectral_cot = (partial.astype(f32).sum(axis=0) * scale[:, None]).astype(bf16)
    every_cot = jnp.broadcast_to(spectral_cot[None], (SNAPS, MODES, 2 * CO))
    every_cot = lax.all_to_all(every_cot, "dp", 0, 0, tiled=True)
    state = (2 * OWN * MODES, CO)
    weight = master.reshape(state)
    got = mix(every_cot, weight, spectrum.reshape(2 * MODES, CI))
    got = lax.all_to_all(got, "dp", 0, 0, tiled=True)
    modes = lax.all_to_all(turn(got), ("sx", "sy"), 0, 0, tiled=True)
    input_grad, *states = finish(
        place, modes, every_cot, got, weight, moment1.reshape(state), moment2.reshape(state)
    )
    return (input_grad.reshape(cotangent.shape), *(s.reshape(master.shape) for s in states))


def solution(mesh):
    grid = P("dp", "sx", "sy", None, None)
    state = P("dp", None, "sx", "sy", None, None)
    in_specs = (grid, P(None, "dp", "sx", "sy", None, None), state, state, state)
    out_specs = (grid, state, state, state)
    return jax.shard_map(shards, mesh=mesh, in_specs=in_specs, out_specs=out_specs, check_vma=False)
```

time: 82.8 us -> 75.8 us (0.915)
  blocking collectives: 55.3 us -> 69 us
  waiting for transfers between devices: 8.04 us -> 0 us
  starting transfers between devices: 5.66 us -> 0 us
  local copies, waits for them, and re-layouts: 3.85 us -> 0.05 us
  Pallas kernels: 7.95 us -> 5.65 us
    all_to_all x0 -> x1, blocking collectives: none -> 13.8 us  [shards(): modes = lax.all_to_all(turn(got), ('sx', 'sy'), 0, 0, tiled=True)]
    all_to_all x1 -> x0, waiting for transfers between devices: 8.04 us -> none  [shards(): modes = lax.all_to_all(turn(got), ('sx', 'sy'), 0, 0, tiled=True)]
    all_to_all x1 -> x0, starting transfers between devices: 5.66 us -> none  [shards(): modes = lax.all_to_all(turn(got), ('sx', 'sy'), 0, 0, tiled=True)]
    unnamed x23 -> x12, local copies, waits for them, and re-layouts: 3.31 us -> 0.03 us
    pallas_call x3 -> x2, Pallas kernels: 4.8 us -> 2.62 us  [the longest x1 2.3 us: finish(): pl.pallas_call(finish_kernel, out_shape=[jax.ShapeDtypeStruct((LX, CELLS,...]
  transfers between devices with their start and end apart: 1 -> 0, of which waited for: 1 -> 0; matrix products, arithmetic and copies ran while one was open for 0% -> 0% of each run, Pallas kernels for 1% -> 0%
where the time goes in v2:
time: 75.8 us; the launch traced here: 75.5 us
  blocking collectives  69 us (91%)
  Pallas kernels  5.65 us (7%)
    all_to_all x1, blocking collectives, shards(): every_cot = lax.all_to_all(every_cot, 'dp', 0, 0, tiled=True)  22.3 us
    all_to_all x1, blocking collectives, shards(): partial = lax.all_to_all(partial, ('sx', 'sy'), 0, 0, tiled=True)  18.3 us
    all_to_all x1, blocking collectives, shards(): got = lax.all_to_all(got, 'dp', 0, 0, tiled=True)  14.6 us
    all_to_all x1, blocking collectives, shards(): modes = lax.all_to_all(turn(got), ('sx', 'sy'), 0, 0, tiled=True)  13.8 us
    pallas_call x1, Pallas kernels, analyse(): pl.pallas_call(analyse_kernel, out_shape=jax.ShapeDtypeStruct((GROUP, MOD...  2.76 us
    pallas_call x1, Pallas kernels, finish(): pl.pallas_call(finish_kernel, out_shape=[jax.ShapeDtypeStruct((LX, CELLS,...  2.3 us

profile of v2, /device:TPU:1, one launch (start us, length us, event | category | flops | bytes accessed | tf_op | source)
XLA Modules:
  0.0 75.5 jit_solution(2383356684452766663)
XLA Ops:
  0.6 0.0 copy-start.5
  0.6 0.0 copy-start.1
  0.7 0.0 copy-start.4
  0.7 0.1 pad_add_fusion.place
  0.7 0.0 copy-start
  0.7 0.0 copy-start.2
  0.7 0.0 copy-start.3
  0.8 2.8 %analyse.1 = bf16[16,16,256]{2,1,0:T(8,128)(2,1)S(1)} custom-call(s32[2]{0:T(128)S(1)} %pad_add_fusion.place, bf16[12,576,128]{2,1,0:T(8,128)(2,1)} %bitcast.16, bf16[128,576]{1,0:T(8,128)(2,1)} %constant.15.clone.table_hbm), custom_call_target="tpu_custom_call" | custom-call | tf_op jit(solution)/shard_map/analyse/pallas_call | solution.py:149
  3.5 18.3 %all_to_all.20 = bf16[16,16,256]{2,1,0:T(8,128)(2,1)S(1)} all-to-all(bf16[16,16,256]{2,1,0:T(8,128)(2,1)S(1)} %analyse.1), channel_id=1, replica_groups=mesh['dp'=32,'sx'=4,'sy'=4] {'sx','sy'}, dimensions={0} | all-to-all | bytes 262144 | tf_op jit(solution)/shard_map/all_to_all | solution.py:336
  21.8 0.0 copy-done.5
  21.8 0.1 multiply_convert_fusion
  21.9 22.3 %all_to_all.21.cot = bf16[32,16,256]{2,1,0:T(8,128)(2,1)S(1)} all-to-all(bf16[32,16,256]{2,1,0:T(8,128)(2,1)S(1)} %broadcast_in_dim.2), channel_id=1, replica_groups=mesh['dp'=32,'sx'=4,'sy'=4] {'dp'}, dimensions={0} | all-to-all | bytes 524288 | tf_op jit(solution)/shard_map/all_to_all | solution.py:340
  44.2 0.0 copy-done.1
  44.2 0.0 copy-done.4
  44.2 0.3 mix.1
  44.6 14.6 %all_to_all.22.got = bf16[32,2,128]{2,1,0:T(2,128)(2,1)S(1)} all-to-all(bf16[32,2,128]{2,1,0:T(2,128)(2,1)S(1)} %mix.1), channel_id=1, replica_groups=mesh['dp'=32,'sx'=4,'sy'=4] {'dp'}, dimensions={0} | all-to-all | bytes 32768 | tf_op jit(solution)/shard_map/all_to_all | solution.py:344
  59.2 0.3 turn.1
  59.5 13.8 %all_to_all.23.modes = bf16[16,32,128]{2,1,0:T(8,128)(2,1)S(1)} all-to-all(bf16[16,32,128]{2,1,0:T(8,128)(2,1)S(1)} %turn.1), channel_id=1, replica_groups=mesh['dp'=32,'sx'=4,'sy'=4] {'sx','sy'}, dimensions={0} | all-to-all | bytes 262144 | tf_op jit(solution)/shard_map/all_to_all | solution.py:345
  73.2 0.0 copy-done
  73.2 0.0 copy-done.2
  73.2 0.0 copy-done.3
  73.2 2.3 %finish.1 = (bf16[12,576,128]{2,1,0:T(8,128)(2,1)}, f32[128,128]{1,0:T(8,128)}, f32[128,128]{1,0:T(8,128)}, f32[128,128]{1,0:T(8,128)}) custom-call(s32[2]{0:T(128)S(1)} %pad_add_fusion.place, bf16[16,32,128]{2,1,0:T(8,128)(2,1)S(1)} %all_to_all.23.modes, bf16[576,192]{1,0:T(8,128)(2,1)S(1)} %copy-done, bf16[32,16,256]{2,1,0:T(8,128)(2,1)S(1)} %all_to_all.21.cot, ...), custom_call_target="tpu_custom_call" | custom-call | tf_op jit(solution)/shard_map/finish/pallas_call | solution.py:315
  (2 shorter events, 0.0 us)
Async XLA Ops:
  0.6 21.2 %copy-start.5 = (f32[16]{0:T(128)S(1)}, f32[16]{0:T(128)}, u32[]{:S(2)}) copy-start(f32[16]{0:T(128)} %constant.23) | copy-start | bytes 196
  0.6 43.6 %copy-start.1 = (f32[4,2,2,2,4,128]{5,4,3,2,1,0:T(4,128)S(1)}, f32[4,2,2,2,4,128]{5,4,3,2,1,0:T(4,128)}, u32[]{:S(2)}) copy-start(f32[4,2,2,2,4,128]{5,4,3,2,1,0:T(4,128)} %param.10) | copy-start | bytes 196612
  0.7 43.6 %copy-start.4 = (bf16[2,1,2,2,4,128]{5,4,3,2,1,0:T(4,128)(2,1)S(1)}, bf16[2,1,2,2,4,128]{5,4,3,2,1,0:T(4,128)(2,1)}, u32[]{:S(2)}) copy-start(bf16[2,1,2,2,4,128]{5,4,3,2,1,0:T(4,128)(2,1)} %param.9) | copy-start | bytes 24580
  0.7 72.5 %copy-start = (bf16[576,192]{1,0:T(8,128)(2,1)S(1)}, bf16[576,192]{1,0:T(8,128)(2,1)}, u32[]{:S(2)}) copy-start(bf16[576,192]{1,0:T(8,128)(2,1)} %constant.17.clone.table) | copy-start | bytes 663556
  0.7 72.5 %copy-start.2 = (f32[4,2,2,2,4,128]{5,4,3,2,1,0:T(4,128)S(1)}, f32[4,2,2,2,4,128]{5,4,3,2,1,0:T(4,128)}, u32[]{:S(2)}) copy-start(f32[4,2,2,2,4,128]{5,4,3,2,1,0:T(4,128)} %param.11) | copy-start | bytes 196612
  0.7 72.5 %copy-start.3 = (f32[4,2,2,2,4,128]{5,4,3,2,1,0:T(4,128)S(1)}, f32[4,2,2,2,4,128]{5,4,3,2,1,0:T(4,128)}, u32[]{:S(2)}) copy-start(f32[4,2,2,2,4,128]{5,4,3,2,1,0:T(4,128)} %param.12) | copy-start | bytes 196612

commit v3 on v2

--- a/solution.py
+++ b/solution.py
@@ -70,7 +70,9 @@
     y_cos, y_sin = np.cos(y_angle), np.sin(y_angle)
     real = np.einsum("ym,zl->mlyz", y_cos, z_cos) + np.einsum("ym,zl->mlyz", y_sin, z_sin)
     imag = np.einsum("ym,zl->mlyz", y_cos, z_sin) - np.einsum("ym,zl->mlyz", y_sin, z_cos)
-    return np.concatenate(high_low(np.stack([real, imag]).reshape(2 * ROWS, CELLS)), axis=0)
+    scale = norm * np.where(np.arange(MZ) > 0, 2.0, 1.0)[:, None, None]
+    table = (np.stack([real, imag]) * scale).reshape(2 * ROWS, CELLS)
+    return np.concatenate(high_low(table), axis=0)
 
 
 def synthesise_table():
@@ -92,16 +94,15 @@
 
 
 def analyse_kernel(place, cot_hbm, table_hbm, out, cot, table, total, sems):
-    chunks = LX // CHUNK
-    copies = [pltpu.make_async_copy(table_hbm, table, sems.at[chunks])]
-    for n in range(chunks):
-        part = pl.ds(n * CHUNK, CHUNK)
-        copies.append(pltpu.make_async_copy(cot_hbm.at[part], cot.at[part], sems.at[n]))
+    copies = [pltpu.make_async_copy(table_hbm, table, sems.at[0])]
+    for n, part in enumerate((pl.ds(0, CHUNK), pl.ds(CHUNK, LX - CHUNK))):
+        copies.append(pltpu.make_async_copy(cot_hbm.at[part], cot.at[part], sems.at[1 + n]))
     for copy in copies:
         copy.start()
     copies[0].wait()
-    for n in range(chunks):
-        copies[1 + n].wait()
+    for n in range(LX // CHUNK):
+        if n < 2:
+            copies[1 + n].wait()
         real, imag = [], []
         for x in range(n * CHUNK, (n + 1) * CHUNK, 2):
             pair = jnp.concatenate([cot[x], cot[x + 1]], axis=1)
@@ -159,7 +160,7 @@
             pltpu.VMEM((LX, CELLS, CO), bf16),
             pltpu.VMEM((4 * ROWS, CELLS), bf16),
             pltpu.VMEM((MX, 2, ROWS, CO), f32),
-            pltpu.SemaphoreType.DMA((LX // CHUNK + 1,)),
+            pltpu.SemaphoreType.DMA((3,)),
         ],
         compiler_params=pltpu.CompilerParams(vmem_limit_bytes=24 * 2**20),
         name="analyse",
@@ -334,8 +335,7 @@
     place = jnp.stack([lax.axis_index("sx"), lax.axis_index("sy")]).astype(jnp.int32)
     partial = analyse(place, cotangent.reshape(LX, CELLS, CO))
     partial = lax.all_to_all(partial, ("sx", "sy"), 0, 0, tiled=True)
-    scale = norm * np.tile(np.array([1.0, 2.0, 2.0, 2.0], np.float32), MODES // MZ)
-    spectral_cot = (partial.astype(f32).sum(axis=0) * scale[:, None]).astype(bf16)
+    spectral_cot = partial.astype(f32).sum(axis=0).astype(bf16)
     every_cot = jnp.broadcast_to(spectral_cot[None], (SNAPS, MODES, 2 * CO))
     every_cot = lax.all_to_all(every_cot, "dp", 0, 0, tiled=True)
     state = (2 * OWN * MODES, CO)

time: 75.8 us -> 75.5 us (level)
  no operation moved by 1% of the time
where the time goes in v3:
time: 75.5 us; the launch traced here: 75.3 us
  blocking collectives  68.9 us (91%)
  Pallas kernels  5.5 us (7%)
    all_to_all x1, blocking collectives, shards(): every_cot = lax.all_to_all(every_cot, 'dp', 0, 0, tiled=True)  22.3 us
    all_to_all x1, blocking collectives, shards(): partial = lax.all_to_all(partial, ('sx', 'sy'), 0, 0, tiled=True)  18.3 us
    all_to_all x1, blocking collectives, shards(): got = lax.all_to_all(got, 'dp', 0, 0, tiled=True)  14.6 us
    all_to_all x1, blocking collectives, shards(): modes = lax.all_to_all(turn(got), ('sx', 'sy'), 0, 0, tiled=True)  13.7 us
    pallas_call x1, Pallas kernels, analyse(): pl.pallas_call(analyse_kernel, out_shape=jax.ShapeDtypeStruct((GROUP, MOD...  2.6 us
    pallas_call x1, Pallas kernels, finish(): pl.pallas_call(finish_kernel, out_shape=[jax.ShapeDtypeStruct((LX, CELLS,...  2.3 us

profile of v3, /device:TPU:1, one launch (start us, length us, event | category | flops | bytes accessed | tf_op | source)
XLA Modules:
  0.0 75.3 jit_solution(7903411456986293592)
XLA Ops:
  0.6 0.0 copy-start.1
  0.6 0.0 copy-start.4
  0.7 0.1 pad_add_fusion.place
  0.7 0.0 copy-start
  0.7 0.0 copy-start.2
  0.7 0.0 copy-start.3
  0.7 2.6 %analyse.1 = bf16[16,16,256]{2,1,0:T(8,128)(2,1)S(1)} custom-call(s32[2]{0:T(128)S(1)} %pad_add_fusion.place, bf16[12,576,128]{2,1,0:T(8,128)(2,1)} %bitcast.16, bf16[128,576]{1,0:T(8,128)(2,1)} %constant.14.clone.table_hbm), custom_call_target="tpu_custom_call" | custom-call | tf_op jit(solution)/shard_map/analyse/pallas_call | solution.py:150
  3.3 18.3 %all_to_all.20 = bf16[16,16,256]{2,1,0:T(8,128)(2,1)S(1)} all-to-all(bf16[16,16,256]{2,1,0:T(8,128)(2,1)S(1)} %analyse.1), channel_id=1, replica_groups=mesh['dp'=32,'sx'=4,'sy'=4] {'sx','sy'}, dimensions={0} | all-to-all | bytes 262144 | tf_op jit(solution)/shard_map/all_to_all | solution.py:337
  21.7 22.3 %all_to_all.21.cot = bf16[32,16,256]{2,1,0:T(8,128)(2,1)S(1)} all-to-all(bf16[32,16,256]{2,1,0:T(8,128)(2,1)S(1)} %broadcast_in_dim.2), channel_id=1, replica_groups=mesh['dp'=32,'sx'=4,'sy'=4] {'dp'}, dimensions={0} | all-to-all | bytes 524288 | tf_op jit(solution)/shard_map/all_to_all | solution.py:340
  44.0 0.0 copy-done.1
  44.0 0.0 copy-done.4
  44.0 0.3 mix.1
  44.3 14.6 %all_to_all.22.got = bf16[32,2,128]{2,1,0:T(2,128)(2,1)S(1)} all-to-all(bf16[32,2,128]{2,1,0:T(2,128)(2,1)S(1)} %mix.1), channel_id=1, replica_groups=mesh['dp'=32,'sx'=4,'sy'=4] {'dp'}, dimensions={0} | all-to-all | bytes 32768 | tf_op jit(solution)/shard_map/all_to_all | solution.py:344
  58.9 0.3 turn.1
  59.2 13.7 %all_to_all.23.modes = bf16[16,32,128]{2,1,0:T(8,128)(2,1)S(1)} all-to-all(bf16[16,32,128]{2,1,0:T(8,128)(2,1)S(1)} %turn.1), channel_id=1, replica_groups=mesh['dp'=32,'sx'=4,'sy'=4] {'sx','sy'}, dimensions={0} | all-to-all | bytes 262144 | tf_op jit(solution)/shard_map/all_to_all | solution.py:345
  73.0 0.0 copy-done
  73.0 0.0 copy-done.2
  73.0 0.0 copy-done.3
  73.0 2.3 %finish.1 = (bf16[12,576,128]{2,1,0:T(8,128)(2,1)}, f32[128,128]{1,0:T(8,128)}, f32[128,128]{1,0:T(8,128)}, f32[128,128]{1,0:T(8,128)}) custom-call(s32[2]{0:T(128)S(1)} %pad_add_fusion.place, bf16[16,32,128]{2,1,0:T(8,128)(2,1)S(1)} %all_to_all.23.modes, bf16[576,192]{1,0:T(8,128)(2,1)S(1)} %copy-done, bf16[32,16,256]{2,1,0:T(8,128)(2,1)S(1)} %all_to_all.21.cot, ...), custom_call_target="tpu_custom_call" | custom-call | tf_op jit(solution)/shard_map/finish/pallas_call | solution.py:316
  (2 shorter events, 0.0 us)
Async XLA Ops:
  0.6 43.3 %copy-start.1 = (f32[4,2,2,2,4,128]{5,4,3,2,1,0:T(4,128)S(1)}, f32[4,2,2,2,4,128]{5,4,3,2,1,0:T(4,128)}, u32[]{:S(2)}) copy-start(f32[4,2,2,2,4,128]{5,4,3,2,1,0:T(4,128)} %param.9) | copy-start | bytes 196612
  0.6 43.3 %copy-start.4 = (bf16[2,1,2,2,4,128]{5,4,3,2,1,0:T(4,128)(2,1)S(1)}, bf16[2,1,2,2,4,128]{5,4,3,2,1,0:T(4,128)(2,1)}, u32[]{:S(2)}) copy-start(bf16[2,1,2,2,4,128]{5,4,3,2,1,0:T(4,128)(2,1)} %param.8) | copy-start | bytes 24580
  0.7 72.2 %copy-start = (bf16[576,192]{1,0:T(8,128)(2,1)S(1)}, bf16[576,192]{1,0:T(8,128)(2,1)}, u32[]{:S(2)}) copy-start(bf16[576,192]{1,0:T(8,128)(2,1)} %constant.15.clone.table) | copy-start | bytes 663556
  0.7 72.2 %copy-start.2 = (f32[4,2,2,2,4,128]{5,4,3,2,1,0:T(4,128)S(1)}, f32[4,2,2,2,4,128]{5,4,3,2,1,0:T(4,128)}, u32[]{:S(2)}) copy-start(f32[4,2,2,2,4,128]{5,4,3,2,1,0:T(4,128)} %param.10) | copy-start | bytes 196612
  0.7 72.2 %copy-start.3 = (f32[4,2,2,2,4,128]{5,4,3,2,1,0:T(4,128)S(1)}, f32[4,2,2,2,4,128]{5,4,3,2,1,0:T(4,128)}, u32[]{:S(2)}) copy-start(f32[4,2,2,2,4,128]{5,4,3,2,1,0:T(4,128)} %param.11) | copy-start | bytes 196612

commit v4 on v3

--- a/solution.py
+++ b/solution.py
@@ -33,6 +33,7 @@
 GROUP = 16
 SNAPS = 32
 OWN = 4
+CORES = 2
 CHUNK = 4
 
 bf16 = jnp.bfloat16
@@ -197,14 +198,16 @@
         channel_of(OWN * SNAPS), spec[...], (((1,), (1,)), ((), ())), preferred_element_type=f32
     )
     pieces = [turned[i * SNAPS : (i + 1) * SNAPS] for i in range(OWN)]
-    out[:, 0, :] = grad.astype(bf16)
-    out[:, 1, :] = jnp.concatenate(pieces, axis=1).astype(bf16)
+    grad, sent = grad.astype(bf16), jnp.concatenate(pieces, axis=1).astype(bf16)
+    for core in range(CORES):
+        out[:, core, 0, :] = grad
+        out[:, core, 1, :] = sent
 
 
 def mix(cot, master, spec):
     return pl.pallas_call(
         mix_kernel,
-        out_shape=jax.ShapeDtypeStruct((SNAPS, 2, 2 * OWN * MODES), bf16),
+        out_shape=jax.ShapeDtypeStruct((SNAPS, CORES, 2, 2 * OWN * MODES), bf16),
         in_specs=[pl.BlockSpec(memory_space=pltpu.VMEM)] * 3,
         out_specs=pl.BlockSpec(memory_space=pltpu.VMEM),
         compiler_params=pltpu.CompilerParams(vmem_limit_bytes=24 * 2**20),
@@ -214,18 +217,20 @@
 
 def turn_kernel(got, out):
     width = 2 * MODES
-    grad = got[:, 0, :]
-    stacked = jnp.concatenate([grad[:, i * width : (i + 1) * width] for i in range(OWN)], axis=0)
-    turned = lax.dot_general(
-        stacked, channel_of(OWN * SNAPS), (((0,), (0,)), ((), ())), preferred_element_type=f32
-    )
-    out[...] = jnp.broadcast_to(turned.astype(bf16)[None], out.shape)
+    for core in range(CORES):
+        grad = got[:, core, 0, :]
+        stacked = jnp.concatenate([grad[:, i * width : (i + 1) * width] for i in range(OWN)], axis=0)
+        turned = lax.dot_general(
+            stacked, channel_of(OWN * SNAPS), (((0,), (0,)), ((), ())), preferred_element_type=f32
+        )
+        shape = (GROUP // CORES, width, CI)
+        out[:, core * width : (core + 1) * width, :] = jnp.broadcast_to(turned.astype(bf16)[None], shape)
 
 
 def turn(got):
     return pl.pallas_call(
         turn_kernel,
-        out_shape=jax.ShapeDtypeStruct((GROUP, 2 * MODES, CI), bf16),
+        out_shape=jax.ShapeDtypeStruct((GROUP // CORES, CORES * 2 * MODES, CI), bf16),
         in_specs=[pl.BlockSpec(memory_space=pltpu.VMEM)],
         out_specs=pl.BlockSpec(memory_space=pltpu.VMEM),
         compiler_params=pltpu.CompilerParams(vmem_limit_bytes=24 * 2**20),
@@ -233,9 +238,9 @@
     )(got)
 
 
-def adam_step(cot, got, master, moment1, moment2):
+def adam_step(place, cot, got, master, moment1, moment2):
     rows, cols = SNAPS * MODES, 2 * OWN * MODES
-    spec = got[:, 1, :].astype(f32)
+    spec = jnp.where(place[1] % CORES == 0, got[:, 0, 1, :].astype(f32), got[:, 1, 1, :].astype(f32))
     spread = jnp.broadcast_to(spec[:, None, :], (SNAPS, MODES, cols)).reshape(rows, cols)
     spread = jnp.where(own_mode(rows, cols), spread, 0.0).astype(bf16)
     products = lax.dot_general(
@@ -257,7 +262,10 @@
 def finish_kernel(place, modes, table, cot, got, master, moment1, moment2, *refs):
     out_hbm, *states_hbm = refs[:4]
     out, states, plus, less, sems = refs[4:]
-    parts = [modes[s].astype(f32) for s in range(GROUP)]
+    width = 2 * MODES
+    parts = [
+        modes[s // CORES, s % CORES * width : (s % CORES + 1) * width].astype(f32) for s in range(GROUP)
+    ]
 
     def field(kx):
         x, j = divmod(kx, 2)
@@ -303,7 +311,7 @@
         part = pl.ds(x, 2)
         copies.append(pltpu.make_async_copy(out.at[part], out_hbm.at[part], sems.at[x // 2]))
         copies[-1].start()
-    for n, state in enumerate(adam_step(cot, got, master, moment1, moment2)):
+    for n, state in enumerate(adam_step(place, cot, got, master, moment1, moment2)):
         states[n] = state
         copies.append(pltpu.make_async_copy(states.at[n], states_hbm[n], sems.at[LX // 2 + n]))
         copies[-1].start()
@@ -331,6 +339,15 @@
     )(place, modes, jnp.asarray(synthesise_table()), cot, got, master, moment1, moment2)
 
 
+def planes():
+    dp, core = np.arange(SNAPS)[:, None], np.arange(CORES)
+    return [(4 * dp + CORES * half + core).reshape(-1).tolist() for half in range(2)]
+
+
+def columns():
+    return [list(range(core, GROUP, CORES)) for core in range(CORES)]
+
+
 def shards(cotangent, spectrum, master, moment1, moment2):
     place = jnp.stack([lax.axis_index("sx"), lax.axis_index("sy")]).astype(jnp.int32)
     partial = analyse(place, cotangent.reshape(LX, CELLS, CO))
@@ -341,8 +358,10 @@
     state = (2 * OWN * MODES, CO)
     weight = master.reshape(state)
     got = mix(every_cot, weight, spectrum.reshape(2 * MODES, CI))
-    got = lax.all_to_all(got, "dp", 0, 0, tiled=True)
-    modes = lax.all_to_all(turn(got), ("sx", "sy"), 0, 0, tiled=True)
+    got = got.reshape(SNAPS * CORES, 2, 2 * OWN * MODES)
+    got = lax.all_to_all(got, ("dp", "sy"), 0, 0, tiled=True, axis_index_groups=planes())
+    got = got.reshape(SNAPS, CORES, 2, 2 * OWN * MODES)
+    modes = lax.all_to_all(turn(got), ("sx", "sy"), 0, 0, tiled=True, axis_index_groups=columns())
     input_grad, *states = finish(
         place, modes, every_cot, got, weight, moment1.reshape(state), moment2.reshape(state)
     )

time: 75.5 us -> 73.5 us (0.974)
  blocking collectives: 68.9 us -> 66.3 us
    all_to_all x2, blocking collectives: 28.4 us -> 25.7 us  [the longest x1 16.6 us: shards(): lax.all_to_all(got, ('dp', 'sy'), 0, 0, tiled=True, axis_index_groups=pla...]
where the time goes in v4:
time: 73.5 us; the launch traced here: 72.7 us
  blocking collectives  66.3 us (90%)
  Pallas kernels  5.52 us (8%)
    all_to_all x1, blocking collectives, shards(): every_cot = lax.all_to_all(every_cot, 'dp', 0, 0, tiled=True)  22.3 us
    all_to_all x1, blocking collectives, shards(): partial = lax.all_to_all(partial, ('sx', 'sy'), 0, 0, tiled=True)  18.3 us
    all_to_all x1, blocking collectives, shards(): lax.all_to_all(got, ('dp', 'sy'), 0, 0, tiled=True, axis_index_groups=pla...  16.6 us
    all_to_all x1, blocking collectives, shards(): lax.all_to_all(turn(got), ('sx', 'sy'), 0, 0, tiled=True, axis_index_grou...  9.11 us
    pallas_call x1, Pallas kernels, analyse(): pl.pallas_call(analyse_kernel, out_shape=jax.ShapeDtypeStruct((GROUP, MOD...  2.6 us
    pallas_call x1, Pallas kernels, finish(): pl.pallas_call(finish_kernel, out_shape=[jax.ShapeDtypeStruct((LX, CELLS,...  2.3 us

profile of v4, /device:TPU:1, one launch (start us, length us, event | category | flops | bytes accessed | tf_op | source)
XLA Modules:
  0.0 72.7 jit_solution(11437957608217767336)
XLA Ops:
  0.6 0.0 copy-start.1
  0.6 0.0 copy-start.4
  0.7 0.1 pad_add_fusion.place
  0.7 0.0 copy-start
  0.7 0.0 copy-start.2
  0.7 0.0 copy-start.3
  0.7 2.6 %analyse.1 = bf16[16,16,256]{2,1,0:T(8,128)(2,1)S(1)} custom-call(s32[2]{0:T(128)S(1)} %pad_add_fusion.place, bf16[12,576,128]{2,1,0:T(8,128)(2,1)} %bitcast.21, bf16[128,576]{1,0:T(8,128)(2,1)} %constant.14.clone.table_hbm), custom_call_target="tpu_custom_call" | custom-call | tf_op jit(solution)/shard_map/analyse/pallas_call | solution.py:151
  3.3 18.3 %all_to_all.20 = bf16[16,16,256]{2,1,0:T(8,128)(2,1)S(1)} all-to-all(bf16[16,16,256]{2,1,0:T(8,128)(2,1)S(1)} %analyse.1), channel_id=1, replica_groups=mesh['dp'=32,'sx'=4,'sy'=4] {'sx','sy'}, dimensions={0} | all-to-all | bytes 262144 | tf_op jit(solution)/shard_map/all_to_all | solution.py:354
  21.7 22.3 %all_to_all.21.cot = bf16[32,16,256]{2,1,0:T(8,128)(2,1)S(1)} all-to-all(bf16[32,16,256]{2,1,0:T(8,128)(2,1)S(1)} %broadcast_in_dim.2), channel_id=1, replica_groups=mesh['dp'=32,'sx'=4,'sy'=4] {'dp'}, dimensions={0} | all-to-all | bytes 524288 | tf_op jit(solution)/shard_map/all_to_all | solution.py:357
  44.0 0.0 copy-done.1
  44.0 0.0 copy-done.4
  44.0 0.3 mix.1
  44.3 16.6 %all_to_all.22 = bf16[64,2,128]{2,1,0:T(2,128)(2,1)S(1)} all-to-all(bf16[64,2,128]{2,1,0:T(2,128)(2,1)S(1)} %bitcast.17), channel_id=1, replica_groups={{0,1,16,17,32,33,48,49,64,65,80,81,96,97,112,113,128,129,144,145,160,16..., dimensions={0} | all-to-all | bytes 65536 | tf_op jit(solution)/shard_map/all_to_all | solution.py:362
  61.0 0.3 turn.1
  61.2 9.1 %all_to_all.23.modes = bf16[8,64,128]{2,1,0:T(8,128)(2,1)S(1)} all-to-all(bf16[8,64,128]{2,1,0:T(8,128)(2,1)S(1)} %turn.1), channel_id=1, replica_groups={{0,2,4,6,8,10,12,14},{1,3,5,7,9,11,13,15},{16,18,20,22,24,26,28,30},{17..., dimensions={0} | all-to-all | bytes 262144 | tf_op jit(solution)/shard_map/all_to_all | solution.py:364
  70.4 0.0 copy-done
  70.4 0.0 copy-done.2
  70.4 0.0 copy-done.3
  70.4 2.3 %finish.1 = (bf16[12,576,128]{2,1,0:T(8,128)(2,1)}, f32[128,128]{1,0:T(8,128)}, f32[128,128]{1,0:T(8,128)}, f32[128,128]{1,0:T(8,128)}) custom-call(s32[2]{0:T(128)S(1)} %pad_add_fusion.place, bf16[8,64,128]{2,1,0:T(8,128)(2,1)S(1)} %all_to_all.23.modes, bf16[576,192]{1,0:T(8,128)(2,1)S(1)} %copy-done, bf16[32,16,256]{2,1,0:T(8,128)(2,1)S(1)} %all_to_all.21.cot, ...), custom_call_target="tpu_custom_call" | custom-call | tf_op jit(solution)/shard_map/finish/pallas_call | solution.py:324
  (2 shorter events, 0.0 us)
Async XLA Ops:
  0.6 43.3 %copy-start.1 = (f32[4,2,2,2,4,128]{5,4,3,2,1,0:T(4,128)S(1)}, f32[4,2,2,2,4,128]{5,4,3,2,1,0:T(4,128)}, u32[]{:S(2)}) copy-start(f32[4,2,2,2,4,128]{5,4,3,2,1,0:T(4,128)} %param.9) | copy-start | bytes 196612
  0.6 43.3 %copy-start.4 = (bf16[2,1,2,2,4,128]{5,4,3,2,1,0:T(4,128)(2,1)S(1)}, bf16[2,1,2,2,4,128]{5,4,3,2,1,0:T(4,128)(2,1)}, u32[]{:S(2)}) copy-start(bf16[2,1,2,2,4,128]{5,4,3,2,1,0:T(4,128)(2,1)} %param.8) | copy-start | bytes 24580
  0.7 69.6 %copy-start = (bf16[576,192]{1,0:T(8,128)(2,1)S(1)}, bf16[576,192]{1,0:T(8,128)(2,1)}, u32[]{:S(2)}) copy-start(bf16[576,192]{1,0:T(8,128)(2,1)} %constant.15.clone.table) | copy-start | bytes 663556
  0.7 69.6 %copy-start.2 = (f32[4,2,2,2,4,128]{5,4,3,2,1,0:T(4,128)S(1)}, f32[4,2,2,2,4,128]{5,4,3,2,1,0:T(4,128)}, u32[]{:S(2)}) copy-start(f32[4,2,2,2,4,128]{5,4,3,2,1,0:T(4,128)} %param.10) | copy-start | bytes 196612
  0.7 69.6 %copy-start.3 = (f32[4,2,2,2,4,128]{5,4,3,2,1,0:T(4,128)S(1)}, f32[4,2,2,2,4,128]{5,4,3,2,1,0:T(4,128)}, u32[]{:S(2)}) copy-start(f32[4,2,2,2,4,128]{5,4,3,2,1,0:T(4,128)} %param.11) | copy-start | bytes 196612

commit v5 on v4

--- a/solution.py
+++ b/solution.py
@@ -264,7 +264,8 @@
     out, states, plus, less, sems = refs[4:]
     width = 2 * MODES
     parts = [
-        modes[s // CORES, s % CORES * width : (s % CORES + 1) * width].astype(f32) for s in range(GROUP)
+        modes[s % 4 // CORES * 4 + s // 4, s % CORES * width : (s % CORES + 1) * width].astype(f32)
+        for s in range(GROUP)
     ]
 
     def field(kx):
@@ -345,7 +346,8 @@
 
 
 def columns():
-    return [list(range(core, GROUP, CORES)) for core in range(CORES)]
+    half, run = np.arange(2)[:, None], np.arange(4)
+    return [(4 * run + CORES * half + core).reshape(-1).tolist() for core in range(CORES)]
 
 
 def shards(cotangent, spectrum, master, moment1, moment2):

time: 73.5 us -> 74.1 us (level)
  blocking collectives: 66.3 us -> 67.4 us
    all_to_all x1, blocking collectives: 9.11 us -> 10.2 us  [shards(): lax.all_to_all(turn(got), ('sx', 'sy'), 0, 0, tiled=True, axis_index_grou...]
where the time goes in v5:
time: 74.1 us; the launch traced here: 73.8 us
  blocking collectives  67.4 us (91%)
  Pallas kernels  5.52 us (7%)
    all_to_all x1, blocking collectives, shards(): every_cot = lax.all_to_all(every_cot, 'dp', 0, 0, tiled=True)  22.3 us
    all_to_all x1, blocking collectives, shards(): partial = lax.all_to_all(partial, ('sx', 'sy'), 0, 0, tiled=True)  18.3 us
    all_to_all x1, blocking collectives, shards(): lax.all_to_all(got, ('dp', 'sy'), 0, 0, tiled=True, axis_index_groups=pla...  16.6 us
    all_to_all x1, blocking collectives, shards(): lax.all_to_all(turn(got), ('sx', 'sy'), 0, 0, tiled=True, axis_index_grou...  10.2 us
    pallas_call x1, Pallas kernels, analyse(): pl.pallas_call(analyse_kernel, out_shape=jax.ShapeDtypeStruct((GROUP, MOD...  2.6 us
    pallas_call x1, Pallas kernels, finish(): pl.pallas_call(finish_kernel, out_shape=[jax.ShapeDtypeStruct((LX, CELLS,...  2.3 us

profile of v5, /device:TPU:1, one launch (start us, length us, event | category | flops | bytes accessed | tf_op | source)
XLA Modules:
  0.0 73.8 jit_solution(9673239409693192851)
XLA Ops:
  0.6 0.0 copy-start.1
  0.6 0.0 copy-start.4
  0.7 0.1 pad_add_fusion.place
  0.7 0.0 copy-start
  0.7 0.0 copy-start.2
  0.7 0.0 copy-start.3
  0.7 2.6 %analyse.1 = bf16[16,16,256]{2,1,0:T(8,128)(2,1)S(1)} custom-call(s32[2]{0:T(128)S(1)} %pad_add_fusion.place, bf16[12,576,128]{2,1,0:T(8,128)(2,1)} %bitcast.21, bf16[128,576]{1,0:T(8,128)(2,1)} %constant.14.clone.table_hbm), custom_call_target="tpu_custom_call" | custom-call | tf_op jit(solution)/shard_map/analyse/pallas_call | solution.py:151
  3.3 18.3 %all_to_all.20 = bf16[16,16,256]{2,1,0:T(8,128)(2,1)S(1)} all-to-all(bf16[16,16,256]{2,1,0:T(8,128)(2,1)S(1)} %analyse.1), channel_id=1, replica_groups=mesh['dp'=32,'sx'=4,'sy'=4] {'sx','sy'}, dimensions={0} | all-to-all | bytes 262144 | tf_op jit(solution)/shard_map/all_to_all | solution.py:356
  21.7 22.3 %all_to_all.21.cot = bf16[32,16,256]{2,1,0:T(8,128)(2,1)S(1)} all-to-all(bf16[32,16,256]{2,1,0:T(8,128)(2,1)S(1)} %broadcast_in_dim.2), channel_id=1, replica_groups=mesh['dp'=32,'sx'=4,'sy'=4] {'dp'}, dimensions={0} | all-to-all | bytes 524288 | tf_op jit(solution)/shard_map/all_to_all | solution.py:359
  44.0 0.0 copy-done.1
  44.0 0.0 copy-done.4
  44.0 0.3 mix.1
  44.3 16.6 %all_to_all.22 = bf16[64,2,128]{2,1,0:T(2,128)(2,1)S(1)} all-to-all(bf16[64,2,128]{2,1,0:T(2,128)(2,1)S(1)} %bitcast.17), channel_id=1, replica_groups={{0,1,16,17,32,33,48,49,64,65,80,81,96,97,112,113,128,129,144,145,160,16..., dimensions={0} | all-to-all | bytes 65536 | tf_op jit(solution)/shard_map/all_to_all | solution.py:364
  61.0 0.3 turn.1
  61.2 10.2 %all_to_all.23.modes = bf16[8,64,128]{2,1,0:T(8,128)(2,1)S(1)} all-to-all(bf16[8,64,128]{2,1,0:T(8,128)(2,1)S(1)} %turn.1), channel_id=1, replica_groups={{0,4,8,12,2,6,10,14},{1,5,9,13,3,7,11,15},{16,20,24,28,18,22,26,30},{17..., dimensions={0} | all-to-all | bytes 262144 | tf_op jit(solution)/shard_map/all_to_all | solution.py:366
  71.5 0.0 copy-done
  71.5 0.0 copy-done.2
  71.5 0.0 copy-done.3
  71.5 2.3 %finish.1 = (bf16[12,576,128]{2,1,0:T(8,128)(2,1)}, f32[128,128]{1,0:T(8,128)}, f32[128,128]{1,0:T(8,128)}, f32[128,128]{1,0:T(8,128)}) custom-call(s32[2]{0:T(128)S(1)} %pad_add_fusion.place, bf16[8,64,128]{2,1,0:T(8,128)(2,1)S(1)} %all_to_all.23.modes, bf16[576,192]{1,0:T(8,128)(2,1)S(1)} %copy-done, bf16[32,16,256]{2,1,0:T(8,128)(2,1)S(1)} %all_to_all.21.cot, ...), custom_call_target="tpu_custom_call" | custom-call | tf_op jit(solution)/shard_map/finish/pallas_call | solution.py:325
  (2 shorter events, 0.0 us)
Async XLA Ops:
  0.6 43.3 %copy-start.1 = (f32[4,2,2,2,4,128]{5,4,3,2,1,0:T(4,128)S(1)}, f32[4,2,2,2,4,128]{5,4,3,2,1,0:T(4,128)}, u32[]{:S(2)}) copy-start(f32[4,2,2,2,4,128]{5,4,3,2,1,0:T(4,128)} %param.9) | copy-start | bytes 196612
  0.6 43.3 %copy-start.4 = (bf16[2,1,2,2,4,128]{5,4,3,2,1,0:T(4,128)(2,1)S(1)}, bf16[2,1,2,2,4,128]{5,4,3,2,1,0:T(4,128)(2,1)}, u32[]{:S(2)}) copy-start(bf16[2,1,2,2,4,128]{5,4,3,2,1,0:T(4,128)(2,1)} %param.8) | copy-start | bytes 24580
  0.7 70.8 %copy-start = (bf16[576,192]{1,0:T(8,128)(2,1)S(1)}, bf16[576,192]{1,0:T(8,128)(2,1)}, u32[]{:S(2)}) copy-start(bf16[576,192]{1,0:T(8,128)(2,1)} %constant.15.clone.table) | copy-start | bytes 663556
  0.7 70.8 %copy-start.2 = (f32[4,2,2,2,4,128]{5,4,3,2,1,0:T(4,128)S(1)}, f32[4,2,2,2,4,128]{5,4,3,2,1,0:T(4,128)}, u32[]{:S(2)}) copy-start(f32[4,2,2,2,4,128]{5,4,3,2,1,0:T(4,128)} %param.10) | copy-start | bytes 196612
  0.7 70.8 %copy-start.3 = (f32[4,2,2,2,4,128]{5,4,3,2,1,0:T(4,128)S(1)}, f32[4,2,2,2,4,128]{5,4,3,2,1,0:T(4,128)}, u32[]{:S(2)}) copy-start(f32[4,2,2,2,4,128]{5,4,3,2,1,0:T(4,128)} %param.11) | copy-start | bytes 196612
